TPU v7x, 128 devices: a whole 4x4x4 slice. The times are simulated.
128 devices in a mesh: tm: 4 (over x_hi, core), tile: 32 (over z, y, x_lo).
Axes of the slice: x: 4 (x_hi: 2, x_lo: 2; x = x_hi * 2 + x_lo), y: 4, z: 4, core: 2. Of those that a mesh axis runs over, the one named last changes fastest.
Arguments:
- tokens: bfloat16 [32768, 5120], P(('tm', 'tile')), may hold values from -6 to 6
- head_shift: float32 [5120], replicated, may hold values from -3 to 3
- head_scale: float32 [5120], replicated, may hold values from -3 to 3
- head_weight: bfloat16 [5120, 64], replicated, may hold values from -0.078125 to 0.078125
- head_bias: float32 [64], replicated, may hold values from -3 to 3
- in_weight: bfloat16 [3, 3, 3, 16, 384], replicated, may hold values from -0.3125 to 0.3125
- in_bias: float32 [384], replicated, may hold values from -3 to 3
- gain_one: float32 [384], replicated, may hold values from 0.1 to 1.9
- weight_one: bfloat16 [3, 3, 3, 384, 384], replicated, may hold values from -0.0625 to 0.0625
- bias_one: float32 [384], replicated, may hold values from -3 to 3
- gain_two: float32 [384], replicated, may hold values from 0.1 to 1.9
- weight_two: bfloat16 [3, 3, 3, 384, 384], replicated, may hold values from -0.0625 to 0.0625
- bias_two: float32 [384], replicated, may hold values from -3 to 3
Outputs:
- result: bfloat16 [16, 32, 64, 4, 384], P('tm', 'tile')
All inputs are finite; a program needn't handle non-finite values.
Results may differ from a plain program's by a relative error of at most 0.013.
Values may be sent and summed in bfloat16 or wider, within the bound.
A program may use at most 256 MiB of HBM per device.

v0:
```python
import functools

import jax
import jax.numpy as jnp
from jax import lax
from jax.experimental import pallas as pl
from jax.experimental.pallas import tpu as pltpu
from jax.sharding import PartitionSpec as P

MESH = pl.DeviceIdType.MESH
TF = 4
TH = 4
KC = 32
EXT_F = TF + 2
EXT_R = TH + 2
ODD_BACK, EVEN, ODD, EVEN_ON = range(4)
ALL_ROWS = (0, 1, 2, 3)
ALL_TAPS = (0, 1, 2)

PIECES = {-1: (0, 1, 3), 0: (0, 3, 1), 1: (1, 4, 0), 2: (3, 4, 0), 3: (5, 3, 0), 4: (7, 1, 0)}


def body_kernel(
    tiles,
    blocks,
    tokens,
    shift_ref,
    scale_ref,
    head_w_ref,
    head_b_ref,
    in_w,
    in_b_ref,
    gain_one_ref,
    w_one,
    bias_one_ref,
    gain_two_ref,
    w_two,
    bias_two_ref,
    out_ref,
    tok,
    modulated,
    own,
    got,
    corner,
    w_in,
    w_corner,
    w1,
    w2,
    act_one,
    act_two,
    stream,
    acc,
    tok_sem,
    w_sem,
    in_sem,
    own_send,
    main_recv,
    side_recv,
    row_send,
    row_recv,
    tm_send,
    tm_recv,
    edge_send,
    edge_recv,
):
    me_m = lax.axis_index("tm")
    me_g = lax.axis_index("tile")
    chan = w1.shape[-1]
    depth = tok.shape[1]
    i32 = jnp.int32

    def at(m, g):
        return {"tm": m, "tile": g}

    def row_of(ref):
        return ref[...].reshape(1, ref.shape[0])

    tok_rows = tok.shape[0] // 4
    tok_copies = [
        pltpu.make_async_copy(
            tokens.at[pl.ds(i * tok_rows, tok_rows)],
            tok.at[pl.ds(i * tok_rows, tok_rows)],
            tok_sem.at[i],
        )
        for i in range(4)
    ]
    in_copy = pltpu.make_async_copy(in_w, w_in, in_sem)
    w_copies = [
        [
            pltpu.make_async_copy(src.at[pl.ds(9 * a, 9)], dst.at[pl.ds(9 * a, 9)], w_sem.at[n, a])
            for a in range(3)
        ]
        for n, (src, dst) in enumerate(((w_one, w1), (w_two, w2)))
    ]
    for copy in tok_copies:
        copy.start()
    in_copy.start()

    frame = lax.div(me_g, tiles // TF)
    part = lax.rem(me_g, tiles // TF)
    home = lax.div(me_g, 4)
    place = lax.rem(me_g, 4)

    def target(dm, d):
        g = 4 * part + d
        m = me_m + dm
        inside = (g >= 0) & (g < tiles) & (m < blocks)
        remote = inside if dm else inside & (g != me_g)
        return m, g, remote

    def source(slot, side):
        m = me_m if slot >= TF else me_m - 1
        other = home + jnp.where(place == 0, -1, 1) if side else home
        g = (slot % TF) * (tiles // TF) + other
        inside = m >= 0
        if side:
            inside = (
                inside
                & ((place == 0) | (place == 3))
                & (other >= 0)
                & (other < tiles // TF)
            )
        remote = inside & (g != me_g) if slot >= TF else inside
        return m, g, remote

    has_up = me_g > 0
    has_down = me_g < tiles - 1
    has_prev = me_m > 0
    has_next = me_m < blocks - 1
    sends_edges = has_next & (lax.rem(me_m, 2) == 1)
    passes_edges = has_next & (lax.rem(me_m, 2) == 0)
    gets_edges = has_prev & (lax.rem(me_m, 2) == 0)

    barrier = pltpu.get_barrier_semaphore()

    def greet(m, g, here):
        @pl.when(here)
        def _():
            pl.semaphore_signal(barrier, inc=1, device_id=at(m, g), device_id_type=MESH)

    for slot in range(2 * TF):
        for side in range(2):
            greet(*source(slot, side))
    greet(me_m, me_g - 1, has_up)
    greet(me_m, me_g + 1, has_down)
    greet(me_m - 1, me_g, has_prev)
    greet(me_m - 1, me_g - 1, gets_edges & has_up)
    greet(me_m - 1, me_g + 1, gets_edges & has_down)

    zero_patch = jnp.zeros((KC, got.shape[-1]), jnp.bfloat16)

    @pl.when(jnp.logical_not(has_prev))
    def _():
        for slot in range(TF):
            for pair in range(4):
                got[slot, pair] = zero_patch
        for version in range(4):
            for row in range(EXT_R):
                for f in range(2):
                    act_two[version, f, row] = jnp.zeros((KC, chan), jnp.bfloat16)

    @pl.when(jnp.logical_not(has_up))
    def _():
        for slot in range(2 * TF):
            got[slot, 0] = zero_patch
        for version in range(4):
            for f in range(EXT_F):
                act_two[version, f, 0] = jnp.zeros((KC, chan), jnp.bfloat16)

    @pl.when(jnp.logical_not(has_down))
    def _():
        for slot in range(2 * TF):
            got[slot, 3] = zero_patch
        for version in range(4):
            for f in range(EXT_F):
                act_two[version, f, EXT_R - 1] = jnp.zeros((KC, chan), jnp.bfloat16)

    lanes = 128

    def head_rows(i, carry):
        rows = pl.ds(pl.multiple_of(i * 16, 16), 16)

        def piece(j):
            return tok[rows, j * lanes : (j + 1) * lanes].astype(jnp.float32)

        def over_lanes(term):
            parts = [jnp.zeros((16, lanes), jnp.float32)] * 2
            for j in range(depth // lanes):
                parts[j % 2] = parts[j % 2] + term(j)
            return jnp.sum(parts[0] + parts[1], axis=-1, keepdims=True) * (1.0 / depth)

        average = over_lanes(piece)

        def squared(j):
            centred = piece(j) - average
            return centred * centred

        factor = lax.rsqrt(over_lanes(squared) + 1e-06)
        for j in range(depth // lanes):
            part = pl.ds(j * lanes, lanes)
            normed = (piece(j) - average) * factor * (1.0 + scale_ref[:, part]) + shift_ref[:, part]
            modulated[rows, part] = normed.astype(jnp.bfloat16)
        return carry

    for i in range(4):
        tok_copies[i].wait()
        if i == 3:
            for copy in w_copies[0]:
                copy.start()
        blocks_of = tok_rows // 16
        lax.fori_loop(i * blocks_of, (i + 1) * blocks_of, head_rows, 0, unroll=min(4, blocks_of))
    head_w = head_w_ref[...]
    patches = lax.dot_general(
        modulated[...],
        jnp.concatenate([head_w, head_w], axis=0),
        (((1,), (1,)), ((), ())),
        preferred_element_type=jnp.float32,
    )
    head_b = jnp.concatenate([row_of(head_b_ref)] * 2, axis=1)
    own[...] = (patches + head_b).astype(jnp.bfloat16).reshape(own.shape)

    def patch_copy(n, dm, d):
        m, g, remote = target(dm, d)
        first, count, slot = PIECES[d]
        return remote, pltpu.make_async_remote_copy(
            src_ref=own.at[pl.ds(first, count)],
            dst_ref=got.at[(0 if dm else TF) + frame, pl.ds(slot, count)],
            send_sem=own_send.at[n],
            recv_sem=(side_recv if d in (-1, 4) else main_recv).at[(0 if dm else TF) + frame],
            device_id=at(m, g),
            device_id_type=MESH,
        )

    sends = [(dm, d) for dm in (1, 0) for d in PIECES]
    count = i32(0)
    for dm, d in sends:
        count = count + target(dm, d)[2].astype(i32)
    for here in (has_up, has_down, has_next, sends_edges & has_up, sends_edges & has_down):
        count = count + here.astype(i32)
    pl.semaphore_wait(barrier, count)

    for n, (dm, d) in enumerate(sends):
        remote, copy = patch_copy(n, dm, d)

        @pl.when(remote)
        def _(copy=copy):
            copy.start()

    for d, (first, size, slot) in PIECES.items():

        @pl.when(4 * part + d == me_g)
        def _(first=first, size=size, slot=slot):
            got[TF + frame, pl.ds(slot, size)] = own[pl.ds(first, size)]

    in_copy.wait()
    w_corner[...] = jnp.zeros(w_corner.shape, jnp.bfloat16)
    for a in range(3):
        for parity, middle in ((0, 2), (1, 1)):
            for cell in range(2):
                for s in range(3):
                    for u in range(3):
                        row = s + cell
                        col = u + middle - 1
                        at_k = (row // 2) * 128 + (col // 2) * 64 + (row % 2) * 32 + (col % 2) * 16
                        at_n = (2 * parity + cell) * chan
                        w_corner[a, pl.ds(at_k, 16), pl.ds(at_n, chan)] = w_in[
                            pl.ds(((a * 3 + u) * 3 + s) * 16, 16), :
                        ]

    for slot in range(2 * TF):
        for side in range(2):
            m, g, remote = source(slot, side)
            for d, (first, size, first_slot) in PIECES.items():
                if (d in (-1, 4)) != bool(side):
                    continue
                which = place == d % 4

                @pl.when(remote & which)
                def _(slot=slot, m=m, g=g, first=first, size=size, first_slot=first_slot, side=side):
                    pltpu.make_async_remote_copy(
                        src_ref=own.at[pl.ds(first, size)],
                        dst_ref=got.at[slot, pl.ds(first_slot, size)],
                        send_sem=own_send.at[0],
                        recv_sem=(side_recv if side else main_recv).at[slot],
                        device_id=at(m, g),
                        device_id_type=MESH,
                    ).wait_recv()

    width = got.shape[-1]
    flat = got[...].astype(jnp.float32).reshape(2 * TF * 4 * KC, width)
    lane = lax.broadcasted_iota(i32, flat.shape, 1)
    pair_col = lax.rem(lax.broadcasted_iota(i32, flat.shape, 0), KC)
    back = jnp.where(pair_col == 0, 0.0, pltpu.roll(flat, 1, 0))
    on = jnp.where(pair_col == KC - 1, 0.0, pltpu.roll(flat, flat.shape[0] - 1, 0))
    left = lane < width // 2
    corner[0] = jnp.where(left, back, flat).astype(jnp.bfloat16).reshape(corner.shape[1:])
    corner[1] = jnp.where(left, flat, on).astype(jnp.bfloat16).reshape(corner.shape[1:])

    col_index = lax.broadcasted_iota(i32, (KC, 1), 0)

    def normed_silu(values, gain, keep=None):
        mean = jnp.sum(values * values, axis=-1, keepdims=True) * (1.0 / chan)
        half = values * lax.rsqrt(mean + 1e-06) * gain
        act = half + half * jnp.tanh(half)
        return act if keep is None else act * keep

    def store_act(ref, f, row, parity, act):
        if parity == 0:
            ref[EVEN, f, row] = act.astype(jnp.bfloat16)
            moved = jnp.where(col_index == KC - 1, 0.0, pltpu.roll(act, KC - 1, 0))
            ref[EVEN_ON, f, row] = moved.astype(jnp.bfloat16)
        else:
            ref[ODD, f, row] = act.astype(jnp.bfloat16)
            moved = jnp.where(col_index == 0, 0.0, pltpu.roll(act, 1, 0))
            ref[ODD_BACK, f, row] = moved.astype(jnp.bfloat16)

    gain_one = row_of(gain_one_ref) * 0.5
    in_bias = jnp.concatenate([row_of(in_b_ref)] * 2, axis=1)
    top_keep = has_up.astype(jnp.float32)
    bottom_keep = has_down.astype(jnp.float32)

    def input_frames(pair, carry):
        first = 2 * pair
        frame_keep = ((pair > 0) | has_prev).astype(jnp.float32)
        for parity in range(2):
            taps = []
            for a in range(3):
                for di in range(2):
                    taps.append(
                        corner[parity, pl.ds(first + a, 2), di : di + 3].reshape(2 * 3 * KC, width)
                    )
            raw = jnp.dot(
                jnp.concatenate(taps, axis=1),
                w_corner[:, :, 2 * chan * parity : 2 * chan * (parity + 1)].reshape(
                    6 * width, 2 * chan
                ),
                preferred_element_type=jnp.float32,
            )
            raw = (raw + in_bias).reshape(2, 3, KC, 2 * chan)
            for f in range(2):
                for ci in range(3):
                    for cell in range(2):
                        row = 2 * ci + cell
                        cells = raw[f, ci, :, cell * chan : (cell + 1) * chan].astype(jnp.bfloat16)
                        stream[parity, first + f, row] = cells
                        keep = frame_keep
                        if row == 0:
                            keep = keep * top_keep
                        if row == EXT_R - 1:
                            keep = keep * bottom_keep
                        act = normed_silu(cells.astype(jnp.float32), gain_one, keep)
                        store_act(act_one, first + f, row, parity, act)
        return carry

    lax.fori_loop(0, 3, input_frames, 0)

    def tap(weight, a, u, s):
        return weight[a * 9 + u * 3 + s]

    def cells(field, version, frames, rows, s):
        if rows == ALL_ROWS:
            view = [field[version, f, s : s + TH] for f in frames]
        else:
            view = [field[version, f, v + s][None] for f in frames for v in rows]
        return jnp.concatenate(view, axis=0).reshape(len(frames) * len(rows) * KC, chan)

    def add_pairs(field, weight, a, first, count, rows, taps):
        total = jnp.dot(
            jnp.concatenate(
                [
                    cells(field, v, [first + a + n for n in range(count)], rows, s)
                    for s in taps
                    for v in (EVEN, ODD)
                ],
                axis=1,
            ),
            jnp.concatenate(
                [
                    jnp.concatenate([tap(weight, a, u + 1, s), tap(weight, a, u, s)], axis=1)
                    for s in taps
                    for u in (0, 1)
                ],
                axis=0,
            ),
            preferred_element_type=jnp.float32,
        ).reshape(count, len(rows), KC, 2 * chan)
        for n in range(count):
            if rows == ALL_ROWS:
                acc[first + n] += total[n]
            else:
                for i, v in enumerate(rows):
                    acc[first + n, v] += total[n, i]

    def add_sides(field, weight, rows, taps, groups, outs):
        for version, u, parity in ((ODD_BACK, 0, 0), (EVEN_ON, 2, 1)):
            total = jnp.dot(
                jnp.concatenate(
                    [cells(field, version, frames, rows, s) for frames, _ in groups for s in taps],
                    axis=1,
                ),
                jnp.concatenate(
                    [
                        jnp.concatenate([tap(weight, a, u, s) for a in times], axis=1)
                        for _, times in groups
                        for s in taps
                    ],
                    axis=0,
                ),
                preferred_element_type=jnp.float32,
            ).reshape(len(outs[0]), len(rows), KC, len(outs) * chan)
            part = pl.ds(parity * chan, chan)
            for k, frames in enumerate(outs):
                for n, f in enumerate(frames):
                    added = total[n, :, :, k * chan : (k + 1) * chan]
                    if rows == ALL_ROWS:
                        acc[f, :, :, part] += added
                    else:
                        for i, v in enumerate(rows):
                            acc[f, v, :, part] += added[i]

    def start_acc(bias_ref):
        bias = jnp.concatenate([row_of(bias_ref)] * 2, axis=1)
        acc[...] = jnp.broadcast_to(bias.reshape(1, 1, 1, 2 * chan), acc.shape)

    gain_two = row_of(gain_two_ref) * 0.5

    def conv_one_rows(rows):
        def one_time(a, carry):
            add_pairs(act_one, w1, a, 0, TF, rows, ALL_TAPS)
            return carry

        lax.fori_loop(0, 3, one_time, 0)
        add_sides(
            act_one, w1, rows, ALL_TAPS, [((1, 3), (1, 0)), ((2, 4), (2, 1))], [(0, 2), (1, 3)]
        )
        add_sides(act_one, w1, rows, ALL_TAPS, [((0, 2), (0,))], [(0, 2)])
        add_sides(act_one, w1, rows, ALL_TAPS, [((3, 5), (2,))], [(1, 3)])

        def finish(f, carry):
            for v in rows:
                for parity in range(2):
                    values = acc[f, v, :, parity * chan : (parity + 1) * chan]
                    store_act(act_two, f + 2, v + 1, parity, normed_silu(values, gain_two))
            return carry

        lax.fori_loop(0, TF, finish, 0, unroll=2)

    def row_copy(way):
        frames = pl.ds(2, TF)
        return pltpu.make_async_remote_copy(
            src_ref=act_two.at[pl.ds(EVEN, 2), frames, 1 if way else TH],
            dst_ref=act_two.at[pl.ds(EVEN, 2), frames, EXT_R - 1 if way else 0],
            send_sem=row_send.at[way],
            recv_sem=row_recv.at[way],
            device_id=at(me_m, me_g - 1 if way else me_g + 1),
            device_id_type=MESH,
        )

    def edge_copy(way):
        return pltpu.make_async_remote_copy(
            src_ref=act_two.at[pl.ds(EVEN, 2), pl.ds(TF, 2), 1 if way else TH],
            dst_ref=act_two.at[pl.ds(EVEN, 2), pl.ds(0, 2), EXT_R - 1 if way else 0],
            send_sem=edge_send.at[way],
            recv_sem=edge_recv.at[way],
            device_id=at(me_m + 1, me_g - 1 if way else me_g + 1),
            device_id_type=MESH,
        )

    def pass_copy(way):
        row = EXT_R - 1 if way else 0
        return pltpu.make_async_remote_copy(
            src_ref=act_two.at[pl.ds(EVEN, 2), pl.ds(TF, 2), row],
            dst_ref=act_two.at[pl.ds(EVEN, 2), pl.ds(0, 2), row],
            send_sem=edge_send.at[way],
            recv_sem=edge_recv.at[way],
            device_id=at(me_m + 1, me_g),
            device_id_type=MESH,
        )

    tm_copy = pltpu.make_async_remote_copy(
        src_ref=act_two.at[pl.ds(EVEN, 2), pl.ds(TF, 2), pl.ds(1, TH)],
        dst_ref=act_two.at[pl.ds(EVEN, 2), pl.ds(0, 2), pl.ds(1, TH)],
        send_sem=tm_send.at[0],
        recv_sem=tm_recv.at[0],
        device_id=at(me_m + 1, me_g),
        device_id_type=MESH,
    )
    way_out = (has_down, has_up)
    way_in = (has_up, has_down)

    def widen(f, row):
        even = act_two[EVEN, f, row].astype(jnp.float32)
        moved = jnp.where(col_index == KC - 1, 0.0, pltpu.roll(even, KC - 1, 0))
        act_two[EVEN_ON, f, row] = moved.astype(jnp.bfloat16)
        odd = act_two[ODD, f, row].astype(jnp.float32)
        moved = jnp.where(col_index == 0, 0.0, pltpu.roll(odd, 1, 0))
        act_two[ODD_BACK, f, row] = moved.astype(jnp.bfloat16)

    start_acc(bias_one_ref)
    for copy in w_copies[0]:
        copy.wait()
    for copy in w_copies[1]:
        copy.start()

    conv_one_rows((0, TH - 1))
    for way in range(2):

        @pl.when(way_out[way])
        def _(way=way):
            row_copy(way).start()

        @pl.when(way_out[way] & sends_edges)
        def _(way=way):
            edge_copy(way).start()

    conv_one_rows((1, 2))

    @pl.when(has_next)
    def _():
        tm_copy.start()

    start_acc(bias_two_ref)
    for copy in w_copies[1]:
        copy.wait()

    def conv_two_own(taps):
        for a in range(3):
            add_pairs(act_two, w2, a, 2 - a, TF - 2 + a, ALL_ROWS, taps)
        add_sides(act_two, w2, ALL_ROWS, taps, [((3,), (1, 0)), ((4,), (2, 1))], [(2,), (3,)])
        add_sides(act_two, w2, ALL_ROWS, taps, [((2,), (2, 1))], [(0,), (1,)])
        add_sides(act_two, w2, ALL_ROWS, taps, [((2,), (0,))], [(2,)])
        add_sides(act_two, w2, ALL_ROWS, taps, [((3, 5), (2,))], [(1, 3)])

    conv_two_own((1,))

    for way in range(2):

        @pl.when(way_in[way])
        def _(way=way):
            row_copy(way).wait_recv()

        @pl.when(way_in[way] & passes_edges)
        def _(way=way):
            pass_copy(way).start()

        @pl.when(way_in[way])
        def _(way=way):
            for f in range(TF):
                widen(2 + f, EXT_R - 1 if way else 0)

    conv_two_own((0, 2))

    @pl.when(has_prev)
    def _():
        tm_copy.wait_recv()

    for way in range(2):

        @pl.when(way_in[way] & has_prev)
        def _(way=way):
            edge_copy(way).wait_recv()

    @pl.when(has_prev)
    def _():
        for f in range(2):

            def widen_row(row, carry, f=f):
                widen(f, row)
                return carry

            lax.fori_loop(0, EXT_R, widen_row, 0, unroll=True)

    add_pairs(act_two, w2, 0, 0, 2, ALL_ROWS, ALL_TAPS)
    add_pairs(act_two, w2, 1, 0, 1, ALL_ROWS, ALL_TAPS)
    add_sides(act_two, w2, ALL_ROWS, ALL_TAPS, [((1,), (1, 0))], [(0,), (1,)])
    add_sides(act_two, w2, ALL_ROWS, ALL_TAPS, [((0,), (0,))], [(0,)])

    area = 2 * TH * KC
    to = lax.broadcasted_iota(i32, (area, area), 0)
    of = lax.broadcasted_iota(i32, (area, area), 1)
    order = jnp.where(
        (lax.div(to, 8) == lax.rem(of, KC)) & (lax.rem(to, 8) == lax.div(of, KC)), 1.0, 0.0
    ).astype(jnp.bfloat16)

    def finish_two(f, carry):
        halves = []
        for parity in range(2):
            whole = acc[f, :, :, parity * chan : (parity + 1) * chan] + stream[
                parity, f + 2, 1 : TH + 1
            ].astype(jnp.float32)
            halves.append(whole.astype(jnp.bfloat16).reshape(TH * KC, chan))
        placed = jnp.dot(
            order, jnp.concatenate(halves, axis=0), preferred_element_type=jnp.float32
        )
        out_ref[f, 0] = placed.reshape(2 * KC, TH, chan).astype(jnp.bfloat16)
        return carry

    lax.fori_loop(0, TF, finish_two, 0)

    for n, (dm, d) in enumerate(sends):
        remote, copy = patch_copy(n, dm, d)

        @pl.when(remote)
        def _(copy=copy):
            copy.wait_send()

    @pl.when(has_next)
    def _():
        tm_copy.wait_send()

    for way in range(2):

        @pl.when(way_out[way])
        def _(way=way):
            row_copy(way).wait_send()

        @pl.when(way_out[way] & sends_edges)
        def _(way=way):
            edge_copy(way).wait_send()

        @pl.when(way_in[way] & passes_edges)
        def _(way=way):
            pass_copy(way).wait_send()


def solution(mesh):
    tiles = mesh.shape["tile"]
    blocks = mesh.shape["tm"]

    def body(
        tokens,
        head_shift,
        head_scale,
        head_weight,
        head_bias,
        in_weight,
        in_bias,
        gain_one,
        weight_one,
        bias_one,
        gain_two,
        weight_two,
        bias_two,
    ):
        count, depth = tokens.shape
        chan = weight_one.shape[-1]
        wide = 2 * head_weight.shape[1]
        in_rows = in_weight.shape[0] * in_weight.shape[1] * in_weight.shape[2] * in_weight.shape[3]
        bf16 = jnp.bfloat16
        hbm = pl.BlockSpec(memory_space=pl.ANY)
        vmem = pl.BlockSpec(memory_space=pltpu.VMEM)
        dma = pltpu.SemaphoreType.DMA
        result = pl.pallas_call(
            functools.partial(body_kernel, tiles, blocks),
            out_shape=jax.ShapeDtypeStruct((TF, 1, 2 * KC, TH, chan), bf16),
            in_specs=[
                hbm, vmem, vmem, vmem, vmem, hbm, vmem, vmem, hbm, vmem, vmem, hbm, vmem,
            ],
            out_specs=vmem,
            scratch_shapes=[
                pltpu.VMEM((count, depth), bf16),
                pltpu.VMEM((count, depth), bf16),
                pltpu.VMEM((count // KC, KC, wide), bf16),
                pltpu.VMEM((2 * TF, 4, KC, wide), bf16),
                pltpu.VMEM((2, 2 * TF, 4, KC, wide), bf16),
                pltpu.VMEM((in_rows, chan), bf16),
                pltpu.VMEM((3, 2 * wide, 4 * chan), bf16),
                pltpu.VMEM((27, chan, chan), bf16),
                pltpu.VMEM((27, chan, chan), bf16),
                pltpu.VMEM((4, EXT_F, EXT_R, KC, chan), bf16),
                pltpu.VMEM((4, EXT_F, EXT_R, KC, chan), bf16),
                pltpu.VMEM((2, EXT_F, EXT_R, KC, chan), bf16),
                pltpu.VMEM((TF, TH, KC, 2 * chan), jnp.float32),
                dma((4,)),
                dma((2, 3)),
                dma,
                dma((12,)),
                dma((2 * TF,)),
                dma((2 * TF,)),
                dma((2,)),
                dma((2,)),
                dma((1,)),
                dma((1,)),
                dma((2,)),
                dma((2,)),
            ],
            compiler_params=pltpu.CompilerParams(
                collective_id=0, has_side_effects=True, vmem_limit_bytes=60 * 1024 * 1024
            ),
            name="decode",
        )(
            tokens,
            head_shift[None],
            head_scale[None],
            head_weight.T,
            head_bias,
            in_weight.reshape(in_rows, chan),
            in_bias,
            gain_one,
            weight_one.reshape(27, chan, chan),
            bias_one,
            gain_two,
            weight_two.reshape(27, chan, chan),
            bias_two,
        )
        return result

    in_specs = (P(("tm", "tile"), None), P(), P(), P(), P(), P(), P(), P(), P(), P(), P(), P(), P())
    out_specs = P("tm", "tile", None, None, None)
    return jax.shard_map(body, mesh=mesh, in_specs=in_specs, out_specs=out_specs, check_vma=False)
```

profile of v0, /device:TPU:18, one launch (start us, length us, event | category | flops | bytes accessed | tf_op | source)
XLA Modules:
  0.0 45.7 jit_solution(8882000774476595589)
XLA Ops:
  0.0 43.4 %decode.1 = bf16[4,1,64,4,384]{4,3,2,1,0:T(4,128)(2,1)} custom-call(bf16[256,5120]{1,0:T(8,128)(2,1)} %tokens.1, f32[1,5120]{1,0:T(1,128)} %bitcast.10, f32[1,5120]{1,0:T(1,128)} %bitcast.11, bf16[64,5120]{1,0:T(8,128)(2,1)} %bitcast.8, f32[64]{0:T(128)} %head_b_ref.1, bf16[432,384]{1,0:T(8,128)(2,1)} %bitcast.9, f32[384]{0:T(512)} %in_b_ref.1, ...), custom_call_target="tpu_custom_call" | custom-call | tf_op jit(solution)/shard_map/decode/pallas_call | solution.py:653
  43.4 2.3 %copy.15 = bf16[4,1,64,4,384]{4,3,2,1,0:T(4,128)(2,1)} copy(bf16[4,1,64,4,384]{4,3,2,1,0:T(4,128)(2,1)} %decode.1) | data formatting | bytes 1572864
where the time goes:
time: 45.9 us; the launch traced here: 45.7 us
  Pallas kernels  43.4 us (95%)
  local copies, waits for them, and re-layouts  2.28 us (5%)
    pallas_call x1, Pallas kernels, body(): pl.pallas_call(functools.partial(body_kernel, tiles, blocks), out_shape=j...  43.4 us
    unnamed x1, local copies, waits for them, and re-layouts  2.28 us

commit v1 on v0

--- a/solution.py
+++ b/solution.py
@@ -358,92 +358,69 @@
         return weight[a * 9 + u * 3 + s]
 
     def cells(field, version, frames, rows, s):
-        if rows == ALL_ROWS:
+        if rows is ALL_ROWS:
             view = [field[version, f, s : s + TH] for f in frames]
         else:
             view = [field[version, f, v + s][None] for f in frames for v in rows]
         return jnp.concatenate(view, axis=0).reshape(len(frames) * len(rows) * KC, chan)
 
-    def add_pairs(field, weight, a, first, count, rows, taps):
-        total = jnp.dot(
-            jnp.concatenate(
-                [
-                    cells(field, v, [first + a + n for n in range(count)], rows, s)
-                    for s in taps
-                    for v in (EVEN, ODD)
-                ],
-                axis=1,
-            ),
-            jnp.concatenate(
-                [
-                    jnp.concatenate([tap(weight, a, u + 1, s), tap(weight, a, u, s)], axis=1)
-                    for s in taps
-                    for u in (0, 1)
-                ],
-                axis=0,
-            ),
-            preferred_element_type=jnp.float32,
-        ).reshape(count, len(rows), KC, 2 * chan)
+    def conv(field, weight, terms, rows, taps):
+        def part(versions, outs):
+            return jnp.dot(
+                jnp.concatenate(
+                    [
+                        cells(field, v, frames, rows, s)
+                        for _, frames in terms
+                        for s in taps
+                        for v in versions
+                    ],
+                    axis=1,
+                ),
+                jnp.concatenate(
+                    [
+                        jnp.concatenate([tap(weight, a, out[k], s) for out in outs], axis=1)
+                        for a, _ in terms
+                        for s in taps
+                        for k in range(len(versions))
+                    ],
+                    axis=0,
+                ),
+                preferred_element_type=jnp.float32,
+            )
+
+        even = part((ODD_BACK,), ((0,),))
+        odd = part((EVEN_ON,), ((2,),))
+        both = part((EVEN, ODD), ((1, 2), (0, 1)))
+        total = both + jnp.concatenate([even, odd], axis=1)
+        return total.reshape(len(terms[0][1]), len(rows), KC, 2 * chan)
+
+    def add_conv(field, weight, a, first, count, rows, taps):
+        total = conv(field, weight, [(a, [first + a + n for n in range(count)])], rows, taps)
         for n in range(count):
-            if rows == ALL_ROWS:
+            if rows is ALL_ROWS:
                 acc[first + n] += total[n]
             else:
                 for i, v in enumerate(rows):
                     acc[first + n, v] += total[n, i]
 
-    def add_sides(field, weight, rows, taps, groups, outs):
-        for version, u, parity in ((ODD_BACK, 0, 0), (EVEN_ON, 2, 1)):
-            total = jnp.dot(
-                jnp.concatenate(
-                    [cells(field, version, frames, rows, s) for frames, _ in groups for s in taps],
-                    axis=1,
-                ),
-                jnp.concatenate(
-                    [
-                        jnp.concatenate([tap(weight, a, u, s) for a in times], axis=1)
-                        for _, times in groups
-                        for s in taps
-                    ],
-                    axis=0,
-                ),
-                preferred_element_type=jnp.float32,
-            ).reshape(len(outs[0]), len(rows), KC, len(outs) * chan)
-            part = pl.ds(parity * chan, chan)
-            for k, frames in enumerate(outs):
-                for n, f in enumerate(frames):
-                    added = total[n, :, :, k * chan : (k + 1) * chan]
-                    if rows == ALL_ROWS:
-                        acc[f, :, :, part] += added
-                    else:
-                        for i, v in enumerate(rows):
-                            acc[f, v, :, part] += added[i]
-
     def start_acc(bias_ref):
         bias = jnp.concatenate([row_of(bias_ref)] * 2, axis=1)
         acc[...] = jnp.broadcast_to(bias.reshape(1, 1, 1, 2 * chan), acc.shape)
 
     gain_two = row_of(gain_two_ref) * 0.5
 
+    bias_one = jnp.concatenate([row_of(bias_one_ref)] * 2, axis=1)
+
     def conv_one_rows(rows):
-        def one_time(a, carry):
-            add_pairs(act_one, w1, a, 0, TF, rows, ALL_TAPS)
-            return carry
-
-        lax.fori_loop(0, 3, one_time, 0)
-        add_sides(
-            act_one, w1, rows, ALL_TAPS, [((1, 3), (1, 0)), ((2, 4), (2, 1))], [(0, 2), (1, 3)]
-        )
-        add_sides(act_one, w1, rows, ALL_TAPS, [((0, 2), (0,))], [(0, 2)])
-        add_sides(act_one, w1, rows, ALL_TAPS, [((3, 5), (2,))], [(1, 3)])
-
-        def finish(f, carry):
-            for v in rows:
-                for parity in range(2):
-                    values = acc[f, v, :, parity * chan : (parity + 1) * chan]
+        total = conv(
+            act_one, w1, [(a, [a + f for f in range(TF)]) for a in range(3)], rows, ALL_TAPS
+        )
+        total = total + bias_one
+        for parity in range(2):
+            for f in range(TF):
+                for i, v in enumerate(rows):
+                    values = total[f, i, :, parity * chan : (parity + 1) * chan]
                     store_act(act_two, f + 2, v + 1, parity, normed_silu(values, gain_two))
-            return carry
-
-        lax.fori_loop(0, TF, finish, 0, unroll=2)
 
     def row_copy(way):
         frames = pl.ds(2, TF)
@@ -496,24 +473,26 @@
         moved = jnp.where(col_index == 0, 0.0, pltpu.roll(odd, 1, 0))
         act_two[ODD_BACK, f, row] = moved.astype(jnp.bfloat16)
 
-    start_acc(bias_one_ref)
     for copy in w_copies[0]:
         copy.wait()
     for copy in w_copies[1]:
         copy.start()
 
-    conv_one_rows((0, TH - 1))
-    for way in range(2):
-
-        @pl.when(way_out[way])
-        def _(way=way):
-            row_copy(way).start()
-
-        @pl.when(way_out[way] & sends_edges)
-        def _(way=way):
-            edge_copy(way).start()
-
-    conv_one_rows((1, 2))
+    def conv_one_part(i, carry):
+        conv_one_rows((i, TH - 1 - i))
+        for way in range(2):
+
+            @pl.when((i == 0) & way_out[way])
+            def _(way=way):
+                row_copy(way).start()
+
+            @pl.when((i == 0) & way_out[way] & sends_edges)
+            def _(way=way):
+                edge_copy(way).start()
+
+        return carry
+
+    lax.fori_loop(0, 2, conv_one_part, 0)
 
     @pl.when(has_next)
     def _():
@@ -523,32 +502,33 @@
     for copy in w_copies[1]:
         copy.wait()
 
-    def conv_two_own(taps):
-        for a in range(3):
-            add_pairs(act_two, w2, a, 2 - a, TF - 2 + a, ALL_ROWS, taps)
-        add_sides(act_two, w2, ALL_ROWS, taps, [((3,), (1, 0)), ((4,), (2, 1))], [(2,), (3,)])
-        add_sides(act_two, w2, ALL_ROWS, taps, [((2,), (2, 1))], [(0,), (1,)])
-        add_sides(act_two, w2, ALL_ROWS, taps, [((2,), (0,))], [(2,)])
-        add_sides(act_two, w2, ALL_ROWS, taps, [((3, 5), (2,))], [(1, 3)])
-
-    conv_two_own((1,))
-
-    for way in range(2):
-
-        @pl.when(way_in[way])
-        def _(way=way):
-            row_copy(way).wait_recv()
-
-        @pl.when(way_in[way] & passes_edges)
-        def _(way=way):
-            pass_copy(way).start()
-
-        @pl.when(way_in[way])
-        def _(way=way):
-            for f in range(TF):
-                widen(2 + f, EXT_R - 1 if way else 0)
-
-    conv_two_own((0, 2))
+    def receive_rows():
+        for way in range(2):
+
+            @pl.when(way_in[way])
+            def _(way=way):
+                row_copy(way).wait_recv()
+
+            @pl.when(way_in[way] & passes_edges)
+            def _(way=way):
+                pass_copy(way).start()
+
+            @pl.when(way_in[way])
+            def _(way=way):
+                for f in range(TF):
+                    widen(2 + f, EXT_R - 1 if way else 0)
+
+    def conv_two_part(i, carry):
+
+        @pl.when(i == 1)
+        def _():
+            receive_rows()
+
+        for a in (2, 1, 0):
+            add_conv(act_two, w2, a, 2 - a, TF - 2 + a, (1 - i, 2 + i), ALL_TAPS)
+        return carry
+
+    lax.fori_loop(0, 2, conv_two_part, 0)
 
     @pl.when(has_prev)
     def _():
@@ -570,10 +550,8 @@
 
             lax.fori_loop(0, EXT_R, widen_row, 0, unroll=True)
 
-    add_pairs(act_two, w2, 0, 0, 2, ALL_ROWS, ALL_TAPS)
-    add_pairs(act_two, w2, 1, 0, 1, ALL_ROWS, ALL_TAPS)
-    add_sides(act_two, w2, ALL_ROWS, ALL_TAPS, [((1,), (1, 0))], [(0,), (1,)])
-    add_sides(act_two, w2, ALL_ROWS, ALL_TAPS, [((0,), (0,))], [(0,)])
+    add_conv(act_two, w2, 0, 0, 2, ALL_ROWS, ALL_TAPS)
+    add_conv(act_two, w2, 1, 0, 1, ALL_ROWS, ALL_TAPS)
 
     area = 2 * TH * KC
     to = lax.broadcasted_iota(i32, (area, area), 0)

time: 45.9 us -> 45.4 us (0.989)
  Pallas kernels: 43.4 us -> 42.9 us
    pallas_call x1, Pallas kernels: 43.4 us -> 42.9 us  [body(): pl.pallas_call(functools.partial(body_kernel, tiles, blocks), out_shape=j...]
where the time goes in v1:
time: 45.4 us; the launch traced here: 45.2 us
  Pallas kernels  42.9 us (94%)
  local copies, waits for them, and re-layouts  2.28 us (5%)
    pallas_call x1, Pallas kernels, body(): pl.pallas_call(functools.partial(body_kernel, tiles, blocks), out_shape=j...  42.9 us
    unnamed x1, local copies, waits for them, and re-layouts  2.28 us

profile of v1, /device:TPU:18, one launch (start us, length us, event | category | flops | bytes accessed | tf_op | source)
XLA Modules:
  0.0 45.2 jit_solution(15842217416709109530)
XLA Ops:
  0.0 42.9 %decode.1 = bf16[4,1,64,4,384]{4,3,2,1,0:T(4,128)(2,1)} custom-call(bf16[256,5120]{1,0:T(8,128)(2,1)} %tokens.1, f32[1,5120]{1,0:T(1,128)} %bitcast.10, f32[1,5120]{1,0:T(1,128)} %bitcast.11, bf16[64,5120]{1,0:T(8,128)(2,1)} %bitcast.8, f32[64]{0:T(128)} %head_b_ref.1, bf16[432,384]{1,0:T(8,128)(2,1)} %bitcast.9, f32[384]{0:T(512)} %in_b_ref.1, ...), custom_call_target="tpu_custom_call" | custom-call | tf_op jit(solution)/shard_map/decode/pallas_call | solution.py:631
  42.9 2.3 %copy.15 = bf16[4,1,64,4,384]{4,3,2,1,0:T(4,128)(2,1)} copy(bf16[4,1,64,4,384]{4,3,2,1,0:T(4,128)(2,1)} %decode.1) | data formatting | bytes 1572864

commit v2 on v1

--- a/solution.py
+++ b/solution.py
@@ -147,7 +147,7 @@
     greet(me_m - 1, me_g - 1, gets_edges & has_up)
     greet(me_m - 1, me_g + 1, gets_edges & has_down)
 
-    zero_patch = jnp.zeros((KC, got.shape[-1]), jnp.bfloat16)
+    zero_patch = jnp.zeros(got.shape[2:], jnp.bfloat16)
 
     @pl.when(jnp.logical_not(has_prev))
     def _():
@@ -217,7 +217,9 @@
         preferred_element_type=jnp.float32,
     )
     head_b = jnp.concatenate([row_of(head_b_ref)] * 2, axis=1)
-    own[...] = (patches + head_b).astype(jnp.bfloat16).reshape(own.shape)
+    spread = (patches + head_b).reshape(own.shape[0], KC, own.shape[2])
+    wide_left = lax.broadcasted_iota(i32, own.shape, 2) < own.shape[2] // 2
+    own[...] = jnp.where(wide_left, spread[:, : KC // 2], spread[:, KC // 2 :]).astype(jnp.bfloat16)
 
     def patch_copy(n, dm, d):
         m, g, remote = target(dm, d)
@@ -287,7 +289,12 @@
                     ).wait_recv()
 
     width = got.shape[-1]
-    flat = got[...].astype(jnp.float32).reshape(2 * TF * 4 * KC, width)
+    packed = got[...].astype(jnp.float32).reshape(2 * TF * 4, KC // 2, width)
+    turned = pltpu.roll(packed.reshape(-1, width), width // 2, 1).reshape(packed.shape)
+    low = lax.broadcasted_iota(i32, packed.shape, 2) < width // 2
+    flat = jnp.concatenate(
+        [jnp.where(low, packed, turned), jnp.where(low, turned, packed)], axis=1
+    ).reshape(2 * TF * 4 * KC, width)
     lane = lax.broadcasted_iota(i32, flat.shape, 1)
     pair_col = lax.rem(lax.broadcasted_iota(i32, flat.shape, 0), KC)
     back = jnp.where(pair_col == 0, 0.0, pltpu.roll(flat, 1, 0))
@@ -394,28 +401,39 @@
         total = both + jnp.concatenate([even, odd], axis=1)
         return total.reshape(len(terms[0][1]), len(rows), KC, 2 * chan)
 
-    def add_conv(field, weight, a, first, count, rows, taps):
-        total = conv(field, weight, [(a, [first + a + n for n in range(count)])], rows, taps)
-        for n in range(count):
-            if rows is ALL_ROWS:
-                acc[first + n] += total[n]
-            else:
-                for i, v in enumerate(rows):
-                    acc[first + n, v] += total[n, i]
-
     def start_acc(bias_ref):
         bias = jnp.concatenate([row_of(bias_ref)] * 2, axis=1)
         acc[...] = jnp.broadcast_to(bias.reshape(1, 1, 1, 2 * chan), acc.shape)
 
     gain_two = row_of(gain_two_ref) * 0.5
 
-    bias_one = jnp.concatenate([row_of(bias_one_ref)] * 2, axis=1)
+    bias_one = row_of(bias_one_ref)
+
+    def conv_one_row(row):
+        total = jnp.dot(
+            jnp.concatenate(
+                [
+                    act_one[u : u + 2, a : a + TF, row + s].reshape(2 * TF * KC, chan)
+                    for a in range(3)
+                    for u in range(3)
+                    for s in range(3)
+                ],
+                axis=1,
+            ),
+            w1[...].reshape(27 * chan, chan),
+            preferred_element_type=jnp.float32,
+        )
+        total = (total + bias_one).reshape(2, TF, KC, chan)
+        for parity in range(2):
+            for f in range(TF):
+                act = normed_silu(total[parity, f], gain_two)
+                store_act(act_two, f + 2, row + 1, parity, act)
 
     def conv_one_rows(rows):
         total = conv(
             act_one, w1, [(a, [a + f for f in range(TF)]) for a in range(3)], rows, ALL_TAPS
         )
-        total = total + bias_one
+        total = total + jnp.concatenate([bias_one, bias_one], axis=1)
         for parity in range(2):
             for f in range(TF):
                 for i, v in enumerate(rows):
@@ -478,21 +496,22 @@
     for copy in w_copies[1]:
         copy.start()
 
-    def conv_one_part(i, carry):
-        conv_one_rows((i, TH - 1 - i))
+    def conv_one_edge(i, carry):
+        conv_one_row((TH - 1) * i)
         for way in range(2):
 
-            @pl.when((i == 0) & way_out[way])
+            @pl.when((i == 1 - way) & way_out[way])
             def _(way=way):
                 row_copy(way).start()
 
-            @pl.when((i == 0) & way_out[way] & sends_edges)
+            @pl.when((i == 1 - way) & way_out[way] & sends_edges)
             def _(way=way):
                 edge_copy(way).start()
 
         return carry
 
-    lax.fori_loop(0, 2, conv_one_part, 0)
+    lax.fori_loop(0, 2, conv_one_edge, 0)
+    conv_one_rows((1, 2))
 
     @pl.when(has_next)
     def _():
@@ -502,33 +521,25 @@
     for copy in w_copies[1]:
         copy.wait()
 
-    def receive_rows():
-        for way in range(2):
-
-            @pl.when(way_in[way])
-            def _(way=way):
-                row_copy(way).wait_recv()
-
-            @pl.when(way_in[way] & passes_edges)
-            def _(way=way):
-                pass_copy(way).start()
-
-            @pl.when(way_in[way])
-            def _(way=way):
-                for f in range(TF):
-                    widen(2 + f, EXT_R - 1 if way else 0)
-
-    def conv_two_part(i, carry):
-
-        @pl.when(i == 1)
-        def _():
-            receive_rows()
-
-        for a in (2, 1, 0):
-            add_conv(act_two, w2, a, 2 - a, TF - 2 + a, (1 - i, 2 + i), ALL_TAPS)
-        return carry
-
-    lax.fori_loop(0, 2, conv_two_part, 0)
+    late = [(a, [2 + a, 3 + a]) for a in range(3)]
+    acc[2:4] += conv(act_two, w2, late, ALL_ROWS, (1,))
+
+    for way in range(2):
+
+        @pl.when(way_in[way])
+        def _(way=way):
+            row_copy(way).wait_recv()
+
+        @pl.when(way_in[way] & passes_edges)
+        def _(way=way):
+            pass_copy(way).start()
+
+        @pl.when(way_in[way])
+        def _(way=way):
+            for f in range(TF):
+                widen(2 + f, EXT_R - 1 if way else 0)
+
+    acc[2:4] += conv(act_two, w2, late, ALL_ROWS, (0, 2))
 
     @pl.when(has_prev)
     def _():
@@ -550,8 +561,8 @@
 
             lax.fori_loop(0, EXT_R, widen_row, 0, unroll=True)
 
-    add_conv(act_two, w2, 0, 0, 2, ALL_ROWS, ALL_TAPS)
-    add_conv(act_two, w2, 1, 0, 1, ALL_ROWS, ALL_TAPS)
+    early = [(a, [a, 1 + a]) for a in range(3)]
+    acc[0:2] += conv(act_two, w2, early, ALL_ROWS, ALL_TAPS)
 
     area = 2 * TH * KC
     to = lax.broadcasted_iota(i32, (area, area), 0)
@@ -599,6 +610,18 @@
         @pl.when(way_in[way] & passes_edges)
         def _(way=way):
             pass_copy(way).wait_send()
+
+
+def place_kernel(held, out, stage, sem):
+    loads = [pltpu.make_async_copy(held.at[f], stage.at[f], sem.at[0, f]) for f in range(TF)]
+    stores = [pltpu.make_async_copy(stage.at[f], out.at[f], sem.at[1, f]) for f in range(TF)]
+    for copy in loads:
+        copy.start()
+    for load, store in zip(loads, stores):
+        load.wait()
+        store.start()
+    for copy in stores:
+        copy.wait()
 
 
 def solution(mesh):
@@ -638,8 +661,8 @@
             scratch_shapes=[
                 pltpu.VMEM((count, depth), bf16),
                 pltpu.VMEM((count, depth), bf16),
-                pltpu.VMEM((count // KC, KC, wide), bf16),
-                pltpu.VMEM((2 * TF, 4, KC, wide), bf16),
+                pltpu.VMEM((count // KC, KC // 2, wide), bf16),
+                pltpu.VMEM((2 * TF, 4, KC // 2, wide), bf16),
                 pltpu.VMEM((2, 2 * TF, 4, KC, wide), bf16),
                 pltpu.VMEM((in_rows, chan), bf16),
                 pltpu.VMEM((3, 2 * wide, 4 * chan), bf16),
@@ -681,7 +704,15 @@
             weight_two.reshape(27, chan, chan),
             bias_two,
         )
-        return result
+        return pl.pallas_call(
+            place_kernel,
+            out_shape=jax.ShapeDtypeStruct(result.shape, bf16),
+            in_specs=[hbm],
+            out_specs=hbm,
+            scratch_shapes=[pltpu.VMEM(result.shape, bf16), dma((2, TF))],
+            compiler_params=pltpu.CompilerParams(vmem_limit_bytes=60 * 1024 * 1024),
+            name="place",
+        )(result)
 
     in_specs = (P(("tm", "tile"), None), P(), P(), P(), P(), P(), P(), P(), P(), P(), P(), P(), P())
     out_specs = P("tm", "tile", None, None, None)

time: 45.4 us -> 44.8 us (0.987)
  the two profiles are of different devices: /device:TPU:18 before, /device:TPU:36 now
where the time goes in v2:
time: 44.8 us; the launch traced here: 44.6 us
  Pallas kernels  44.4 us (99%)
    pallas_call x1, Pallas kernels, body(): pl.pallas_call(functools.partial(body_kernel, tiles, blocks), out_shape=j...  42.5 us
    pallas_call x1, Pallas kernels, body(): pl.pallas_call(place_kernel, out_shape=jax.ShapeDtypeStruct(result.shape,...  1.96 us

profile of v2, /device:TPU:36, one launch (start us, length us, event | category | flops | bytes accessed | tf_op | source)
XLA Modules:
  0.0 44.6 jit_solution(182617244808761051)
XLA Ops:
  0.0 42.5 %decode.1.held = bf16[4,1,64,4,384]{4,3,2,1,0:T(4,128)(2,1)} custom-call(bf16[256,5120]{1,0:T(8,128)(2,1)} %tokens.1, f32[1,5120]{1,0:T(1,128)} %bitcast.10, f32[1,5120]{1,0:T(1,128)} %bitcast.11, bf16[64,5120]{1,0:T(8,128)(2,1)} %bitcast.8, f32[64]{0:T(128)} %head_b_ref.1, bf16[432,384]{1,0:T(8,128)(2,1)} %bitcast.9, f32[384]{0:T(512)} %in_b_ref.1, ...), custom_call_target="tpu_custom_call" | custom-call | tf_op jit(solution)/shard_map/decode/pallas_call | solution.py:654
  42.5 2.0 %place.1 = bf16[4,1,64,4,384]{4,3,2,1,0:T(4,128)(2,1)} custom-call(bf16[4,1,64,4,384]{4,3,2,1,0:T(4,128)(2,1)} %decode.1.held), custom_call_target="tpu_custom_call" | custom-call | tf_op jit(solution)/shard_map/place/pallas_call | solution.py:707

commit v3 on v2

--- a/solution.py
+++ b/solution.py
@@ -303,39 +303,46 @@
     corner[0] = jnp.where(left, back, flat).astype(jnp.bfloat16).reshape(corner.shape[1:])
     corner[1] = jnp.where(left, flat, on).astype(jnp.bfloat16).reshape(corner.shape[1:])
 
-    col_index = lax.broadcasted_iota(i32, (KC, 1), 0)
 
     def normed_silu(values, gain, keep=None):
-        mean = jnp.sum(values * values, axis=-1, keepdims=True) * (1.0 / chan)
-        half = values * lax.rsqrt(mean + 1e-06) * gain
-        act = half + half * jnp.tanh(half)
-        return act if keep is None else act * keep
+        factor = lax.rsqrt(jnp.sum(values * values, axis=-1, keepdims=True) * (1.0 / chan) + 1e-06)
+        if keep is not None:
+            factor = factor * keep
+        half = values * factor * gain
+        return half + half * jnp.tanh(half)
+
+    first_eight = lax.broadcasted_iota(i32, (8, chan), 0)
+
+    def moved_on(act):
+        moved = pltpu.roll(act, KC - 1, 0)
+        last = jnp.where(first_eight == 7, 0.0, moved[KC - 8 :])
+        return jnp.concatenate([moved[: KC - 8], last], axis=0)
+
+    def moved_back(act):
+        moved = pltpu.roll(act, 1, 0)
+        return jnp.concatenate([jnp.where(first_eight == 0, 0.0, moved[:8]), moved[8:]], axis=0)
 
     def store_act(ref, f, row, parity, act):
         if parity == 0:
             ref[EVEN, f, row] = act.astype(jnp.bfloat16)
-            moved = jnp.where(col_index == KC - 1, 0.0, pltpu.roll(act, KC - 1, 0))
-            ref[EVEN_ON, f, row] = moved.astype(jnp.bfloat16)
+            ref[EVEN_ON, f, row] = moved_on(act).astype(jnp.bfloat16)
         else:
             ref[ODD, f, row] = act.astype(jnp.bfloat16)
-            moved = jnp.where(col_index == 0, 0.0, pltpu.roll(act, 1, 0))
-            ref[ODD_BACK, f, row] = moved.astype(jnp.bfloat16)
+            ref[ODD_BACK, f, row] = moved_back(act).astype(jnp.bfloat16)
 
     gain_one = row_of(gain_one_ref) * 0.5
     in_bias = jnp.concatenate([row_of(in_b_ref)] * 2, axis=1)
     top_keep = has_up.astype(jnp.float32)
     bottom_keep = has_down.astype(jnp.float32)
-
-    def input_frames(pair, carry):
-        first = 2 * pair
-        frame_keep = ((pair > 0) | has_prev).astype(jnp.float32)
+    prev_keep = has_prev.astype(jnp.float32)
+
+    def input_rows(ci):
         for parity in range(2):
-            taps = []
-            for a in range(3):
-                for di in range(2):
-                    taps.append(
-                        corner[parity, pl.ds(first + a, 2), di : di + 3].reshape(2 * 3 * KC, width)
-                    )
+            taps = [
+                corner[parity, a : a + EXT_F, ci + di].reshape(EXT_F * KC, width)
+                for a in range(3)
+                for di in range(2)
+            ]
             raw = jnp.dot(
                 jnp.concatenate(taps, axis=1),
                 w_corner[:, :, 2 * chan * parity : 2 * chan * (parity + 1)].reshape(
@@ -343,23 +350,22 @@
                 ),
                 preferred_element_type=jnp.float32,
             )
-            raw = (raw + in_bias).reshape(2, 3, KC, 2 * chan)
-            for f in range(2):
-                for ci in range(3):
-                    for cell in range(2):
-                        row = 2 * ci + cell
-                        cells = raw[f, ci, :, cell * chan : (cell + 1) * chan].astype(jnp.bfloat16)
-                        stream[parity, first + f, row] = cells
-                        keep = frame_keep
-                        if row == 0:
-                            keep = keep * top_keep
-                        if row == EXT_R - 1:
-                            keep = keep * bottom_keep
-                        act = normed_silu(cells.astype(jnp.float32), gain_one, keep)
-                        store_act(act_one, first + f, row, parity, act)
-        return carry
-
-    lax.fori_loop(0, 3, input_frames, 0)
+            raw = (raw + in_bias).reshape(EXT_F, KC, 2 * chan)
+            for f in range(EXT_F):
+                for cell in range(2):
+                    row = 2 * ci + cell
+                    values = raw[f, :, cell * chan : (cell + 1) * chan]
+                    if f >= 2 and 1 <= row <= TH:
+                        stream[parity, f - 2, row - 1] = values.astype(jnp.bfloat16)
+                    keep = prev_keep if f < 2 else None
+                    for edge, edge_keep in ((0, top_keep), (EXT_R - 1, bottom_keep)):
+                        if row == edge:
+                            keep = edge_keep if keep is None else keep * edge_keep
+                    act = normed_silu(values, gain_one, keep)
+                    store_act(act_one, f, row, parity, act)
+
+    input_rows(0)
+    input_rows(1)
 
     def tap(weight, a, u, s):
         return weight[a * 9 + u * 3 + s]
@@ -371,74 +377,79 @@
             view = [field[version, f, v + s][None] for f in frames for v in rows]
         return jnp.concatenate(view, axis=0).reshape(len(frames) * len(rows) * KC, chan)
 
-    def conv(field, weight, terms, rows, taps):
-        def part(versions, outs):
-            return jnp.dot(
-                jnp.concatenate(
-                    [
-                        cells(field, v, frames, rows, s)
-                        for _, frames in terms
-                        for s in taps
-                        for v in versions
-                    ],
-                    axis=1,
-                ),
-                jnp.concatenate(
-                    [
-                        jnp.concatenate([tap(weight, a, out[k], s) for out in outs], axis=1)
-                        for a, _ in terms
-                        for s in taps
-                        for k in range(len(versions))
-                    ],
-                    axis=0,
-                ),
-                preferred_element_type=jnp.float32,
-            )
-
-        even = part((ODD_BACK,), ((0,),))
-        odd = part((EVEN_ON,), ((2,),))
-        both = part((EVEN, ODD), ((1, 2), (0, 1)))
-        total = both + jnp.concatenate([even, odd], axis=1)
-        return total.reshape(len(terms[0][1]), len(rows), KC, 2 * chan)
-
-    def start_acc(bias_ref):
-        bias = jnp.concatenate([row_of(bias_ref)] * 2, axis=1)
-        acc[...] = jnp.broadcast_to(bias.reshape(1, 1, 1, 2 * chan), acc.shape)
-
-    gain_two = row_of(gain_two_ref) * 0.5
-
-    bias_one = row_of(bias_one_ref)
-
-    def conv_one_row(row):
-        total = jnp.dot(
+    def product(field, weight, groups, rows, taps):
+        return jnp.dot(
+            jnp.concatenate(
+                [cells(field, version, frames, rows, s) for version, frames, _ in groups for s in taps],
+                axis=1,
+            ),
             jnp.concatenate(
                 [
-                    act_one[u : u + 2, a : a + TF, row + s].reshape(2 * TF * KC, chan)
-                    for a in range(3)
-                    for u in range(3)
-                    for s in range(3)
+                    jnp.concatenate([tap(weight, a, u, s) for a, u in outs], axis=1)
+                    for _, _, outs in groups
+                    for s in taps
                 ],
-                axis=1,
+                axis=0,
             ),
-            w1[...].reshape(27 * chan, chan),
             preferred_element_type=jnp.float32,
         )
-        total = (total + bias_one).reshape(2, TF, KC, chan)
-        for parity in range(2):
-            for f in range(TF):
-                act = normed_silu(total[parity, f], gain_two)
-                store_act(act_two, f + 2, row + 1, parity, act)
-
-    def conv_one_rows(rows):
-        total = conv(
-            act_one, w1, [(a, [a + f for f in range(TF)]) for a in range(3)], rows, ALL_TAPS
-        )
-        total = total + jnp.concatenate([bias_one, bias_one], axis=1)
-        for parity in range(2):
+
+    def conv(field, weight, frames, rows, taps, paired):
+        shape = (len(frames), len(rows), KC, chan)
+        sides = []
+        for version, u in ((ODD_BACK, 0), (EVEN_ON, 2)):
+            if paired:
+                firsts = frames[0::2]
+                half = (len(firsts), len(rows), KC, chan)
+                two = product(
+                    field,
+                    weight,
+                    [(version, [f + n for f in firsts], ((n, u), (n - 1, u))) for n in (1, 2)],
+                    rows,
+                    taps,
+                )
+                one = product(field, weight, [(version, firsts, ((0, u),))], rows, taps)
+                other = product(
+                    field, weight, [(version, [f + 3 for f in firsts], ((2, u),))], rows, taps
+                )
+                one = (one + two[:, :chan]).reshape(half)
+                other = (other + two[:, chan:]).reshape(half)
+                side = jnp.stack([one, other], axis=1)
+            else:
+                side = product(
+                    field,
+                    weight,
+                    [(version, [f + a for f in frames], ((a, u),)) for a in range(3)],
+                    rows,
+                    taps,
+                )
+            sides.append(side.reshape(shape))
+        both = product(
+            field,
+            weight,
+            [
+                (version, [f + a for f in frames], ((a, u + 1), (a, u)))
+                for a in range(3)
+                for version, u in ((EVEN, 0), (ODD, 1))
+            ],
+            rows,
+            taps,
+        )
+        return [
+            both[:, p * chan : (p + 1) * chan].reshape(shape) + sides[p] for p in range(2)
+        ]
+
+    gain_two = row_of(gain_two_ref) * 0.5
+    bias_one = row_of(bias_one_ref)
+    bias_two = row_of(bias_two_ref)
+    own_frames = list(range(TF))
+
+    def act_two_rows(totals, rows):
+        for parity, total in enumerate(totals):
             for f in range(TF):
                 for i, v in enumerate(rows):
-                    values = total[f, i, :, parity * chan : (parity + 1) * chan]
-                    store_act(act_two, f + 2, v + 1, parity, normed_silu(values, gain_two))
+                    act = normed_silu(total[f, i] + bias_one, gain_two)
+                    store_act(act_two, f + 2, v + 1, parity, act)
 
     def row_copy(way):
         frames = pl.ds(2, TF)
@@ -485,44 +496,41 @@
 
     def widen(f, row):
         even = act_two[EVEN, f, row].astype(jnp.float32)
-        moved = jnp.where(col_index == KC - 1, 0.0, pltpu.roll(even, KC - 1, 0))
-        act_two[EVEN_ON, f, row] = moved.astype(jnp.bfloat16)
+        act_two[EVEN_ON, f, row] = moved_on(even).astype(jnp.bfloat16)
         odd = act_two[ODD, f, row].astype(jnp.float32)
-        moved = jnp.where(col_index == 0, 0.0, pltpu.roll(odd, 1, 0))
-        act_two[ODD_BACK, f, row] = moved.astype(jnp.bfloat16)
+        act_two[ODD_BACK, f, row] = moved_back(odd).astype(jnp.bfloat16)
 
     for copy in w_copies[0]:
         copy.wait()
     for copy in w_copies[1]:
         copy.start()
 
-    def conv_one_edge(i, carry):
-        conv_one_row((TH - 1) * i)
-        for way in range(2):
-
-            @pl.when((i == 1 - way) & way_out[way])
-            def _(way=way):
-                row_copy(way).start()
-
-            @pl.when((i == 1 - way) & way_out[way] & sends_edges)
-            def _(way=way):
-                edge_copy(way).start()
-
-        return carry
-
-    lax.fori_loop(0, 2, conv_one_edge, 0)
-    conv_one_rows((1, 2))
+    for row, way in ((0, 1), (TH - 1, 0)):
+        totals = conv(act_one, w1, own_frames, (row,), ALL_TAPS, False)
+        if row == 0:
+            input_rows(2)
+        act_two_rows(totals, (row,))
+
+        @pl.when(way_out[way])
+        def _(way=way):
+            row_copy(way).start()
+
+        @pl.when(way_out[way] & sends_edges)
+        def _(way=way):
+            edge_copy(way).start()
+
+    act_two_rows(conv(act_one, w1, own_frames, (1, 2), ALL_TAPS, True), (1, 2))
 
     @pl.when(has_next)
     def _():
         tm_copy.start()
 
-    start_acc(bias_two_ref)
     for copy in w_copies[1]:
         copy.wait()
 
-    late = [(a, [2 + a, 3 + a]) for a in range(3)]
-    acc[2:4] += conv(act_two, w2, late, ALL_ROWS, (1,))
+    totals = conv(act_two, w2, [2, 3], ALL_ROWS, (1,), True)
+    for parity in range(2):
+        acc[parity] = totals[parity] + bias_two
 
     for way in range(2):
 
@@ -539,7 +547,9 @@
             for f in range(TF):
                 widen(2 + f, EXT_R - 1 if way else 0)
 
-    acc[2:4] += conv(act_two, w2, late, ALL_ROWS, (0, 2))
+    totals = conv(act_two, w2, [2, 3], ALL_ROWS, (0, 2), True)
+    for parity in range(2):
+        acc[parity] += totals[parity]
 
     @pl.when(has_prev)
     def _():
@@ -560,9 +570,6 @@
                 return carry
 
             lax.fori_loop(0, EXT_R, widen_row, 0, unroll=True)
-
-    early = [(a, [a, 1 + a]) for a in range(3)]
-    acc[0:2] += conv(act_two, w2, early, ALL_ROWS, ALL_TAPS)
 
     area = 2 * TH * KC
     to = lax.broadcasted_iota(i32, (area, area), 0)
@@ -571,20 +578,23 @@
         (lax.div(to, 8) == lax.rem(of, KC)) & (lax.rem(to, 8) == lax.div(of, KC)), 1.0, 0.0
     ).astype(jnp.bfloat16)
 
-    def finish_two(f, carry):
-        halves = []
-        for parity in range(2):
-            whole = acc[f, :, :, parity * chan : (parity + 1) * chan] + stream[
-                parity, f + 2, 1 : TH + 1
-            ].astype(jnp.float32)
-            halves.append(whole.astype(jnp.bfloat16).reshape(TH * KC, chan))
+    def finish(f, totals):
+        halves = [
+            (totals[p] + stream[p, f].astype(jnp.float32))
+            .astype(jnp.bfloat16)
+            .reshape(TH * KC, chan)
+            for p in range(2)
+        ]
         placed = jnp.dot(
             order, jnp.concatenate(halves, axis=0), preferred_element_type=jnp.float32
         )
         out_ref[f, 0] = placed.reshape(2 * KC, TH, chan).astype(jnp.bfloat16)
-        return carry
-
-    lax.fori_loop(0, TF, finish_two, 0)
+
+    totals = conv(act_two, w2, [0, 1], ALL_ROWS, ALL_TAPS, True)
+    for f in range(2):
+        finish(2 + f, [acc[p, f] for p in range(2)])
+    for f in range(2):
+        finish(f, [totals[p][f] + bias_two for p in range(2)])
 
     for n, (dm, d) in enumerate(sends):
         remote, copy = patch_copy(n, dm, d)
@@ -612,15 +622,11 @@
             pass_copy(way).wait_send()
 
 
-def place_kernel(held, out, stage, sem):
-    loads = [pltpu.make_async_copy(held.at[f], stage.at[f], sem.at[0, f]) for f in range(TF)]
-    stores = [pltpu.make_async_copy(stage.at[f], out.at[f], sem.at[1, f]) for f in range(TF)]
-    for copy in loads:
+def place_kernel(held, out, sem):
+    copies = [pltpu.make_async_copy(held.at[f], out.at[f], sem.at[f]) for f in range(TF)]
+    for copy in copies:
         copy.start()
-    for load, store in zip(loads, stores):
-        load.wait()
-        store.start()
-    for copy in stores:
+    for copy in copies:
         copy.wait()
 
 
@@ -653,7 +659,7 @@
         dma = pltpu.SemaphoreType.DMA
         result = pl.pallas_call(
             functools.partial(body_kernel, tiles, blocks),
-            out_shape=jax.ShapeDtypeStruct((TF, 1, 2 * KC, TH, chan), bf16),
+            out_shape=pltpu.VMEM((TF, 1, 2 * KC, TH, chan), bf16),
             in_specs=[
                 hbm, vmem, vmem, vmem, vmem, hbm, vmem, vmem, hbm, vmem, vmem, hbm, vmem,
             ],
@@ -670,8 +676,8 @@
                 pltpu.VMEM((27, chan, chan), bf16),
                 pltpu.VMEM((4, EXT_F, EXT_R, KC, chan), bf16),
                 pltpu.VMEM((4, EXT_F, EXT_R, KC, chan), bf16),
-                pltpu.VMEM((2, EXT_F, EXT_R, KC, chan), bf16),
-                pltpu.VMEM((TF, TH, KC, 2 * chan), jnp.float32),
+                pltpu.VMEM((2, TF, TH, KC, chan), bf16),
+                pltpu.VMEM((2, 2, TH, KC, chan), jnp.float32),
                 dma((4,)),
                 dma((2, 3)),
                 dma,
@@ -686,7 +692,7 @@
                 dma((2,)),
             ],
             compiler_params=pltpu.CompilerParams(
-                collective_id=0, has_side_effects=True, vmem_limit_bytes=60 * 1024 * 1024
+                collective_id=0, has_side_effects=True, vmem_limit_bytes=56 * 1024 * 1024
             ),
             name="decode",
         )(
@@ -707,10 +713,9 @@
         return pl.pallas_call(
             place_kernel,
             out_shape=jax.ShapeDtypeStruct(result.shape, bf16),
-            in_specs=[hbm],
+            in_specs=[vmem],
             out_specs=hbm,
-            scratch_shapes=[pltpu.VMEM(result.shape, bf16), dma((2, TF))],
-            compiler_params=pltpu.CompilerParams(vmem_limit_bytes=60 * 1024 * 1024),
+            scratch_shapes=[dma((TF,))],
             name="place",
         )(result)
 

time: 44.8 us -> 43 us (0.960)
  Pallas kernels: 44.4 us -> 41.8 us
  local copies, waits for them, and re-layouts: 0 us -> 0.88 us
    pallas_call x1, Pallas kernels: 42.5 us -> 39.7 us  [body(): pl.pallas_call(functools.partial(body_kernel, tiles, blocks), out_shape=p...]
    unnamed x0 -> x2, local copies, waits for them, and re-layouts: none -> 0.88 us
where the time goes in v3:
time: 43 us; the launch traced here: 42.9 us
  Pallas kernels  41.8 us (97%)
  local copies, waits for them, and re-layouts  0.88 us (2%)
    pallas_call x1, Pallas kernels, body(): pl.pallas_call(functools.partial(body_kernel, tiles, blocks), out_shape=p...  39.7 us
    pallas_call x1, Pallas kernels, body(): pl.pallas_call(place_kernel, out_shape=jax.ShapeDtypeStruct(result.shape,...  2.04 us
    unnamed x2, local copies, waits for them, and re-layouts  0.88 us

profile of v3, /device:TPU:36, one launch (start us, length us, event | category | flops | bytes accessed | tf_op | source)
XLA Modules:
  0.0 42.9 jit_solution(1026475229862474027)
XLA Ops:
  0.0 39.7 %decode.1.held = bf16[4,1,64,4,384]{4,3,2,1,0:T(4,128)(2,1)S(1)} custom-call(bf16[256,5120]{1,0:T(8,128)(2,1)} %tokens.1, f32[1,5120]{1,0:T(1,128)} %bitcast.10, f32[1,5120]{1,0:T(1,128)} %bitcast.11, bf16[64,5120]{1,0:T(8,128)(2,1)} %bitcast.8, f32[64]{0:T(128)} %head_b_ref.1, bf16[432,384]{1,0:T(8,128)(2,1)} %bitcast.9, f32[384]{0:T(512)} %in_b_ref.1, ...), custom_call_target="tpu_custom_call" | custom-call | tf_op jit(solution)/shard_map/decode/pallas_call | solution.py:660
  39.8 0.0 copy-start
  39.8 0.9 %copy-done = bf16[4,1,64,4,384]{4,3,2,1,0:T(4,128)(2,1)} copy-done((bf16[4,1,64,4,384]{4,3,2,1,0:T(4,128)(2,1)}, bf16[4,1,64,4,384]{4,3,2,1,0:T(4,128)(2,1)S(1)}, u32[]{:S(2)}) %copy-start) | copy-done | bytes 786456
  40.6 2.0 %place.1 = bf16[4,1,64,4,384]{4,3,2,1,0:T(4,128)(2,1)} custom-call(bf16[4,1,64,4,384]{4,3,2,1,0:T(4,128)(2,1)} %copy-done), custom_call_target="tpu_custom_call" | custom-call | tf_op jit(solution)/shard_map/place/pallas_call | solution.py:713
Async XLA Ops:
  39.8 0.9 %copy-start = (bf16[4,1,64,4,384]{4,3,2,1,0:T(4,128)(2,1)}, bf16[4,1,64,4,384]{4,3,2,1,0:T(4,128)(2,1)S(1)}, u32[]{:S(2)}) copy-start(bf16[4,1,64,4,384]{4,3,2,1,0:T(4,128)(2,1)S(1)} %decode.1.held) | copy-start | bytes 2359300

commit v4 on v3

--- a/solution.py
+++ b/solution.py
@@ -39,6 +39,7 @@
     out_ref,
     tok,
     modulated,
+    affine,
     own,
     got,
     corner,
@@ -49,6 +50,7 @@
     act_one,
     act_two,
     stream,
+    third,
     acc,
     tok_sem,
     w_sem,
@@ -177,28 +179,29 @@
 
     lanes = 128
 
+    affine[0] = jnp.broadcast_to(1.0 + scale_ref[...], affine.shape[1:])
+    affine[1] = jnp.broadcast_to(shift_ref[...], affine.shape[1:])
+
     def head_rows(i, carry):
         rows = pl.ds(pl.multiple_of(i * 16, 16), 16)
 
         def piece(j):
             return tok[rows, j * lanes : (j + 1) * lanes].astype(jnp.float32)
 
-        def over_lanes(term):
-            parts = [jnp.zeros((16, lanes), jnp.float32)] * 2
-            for j in range(depth // lanes):
-                parts[j % 2] = parts[j % 2] + term(j)
-            return jnp.sum(parts[0] + parts[1], axis=-1, keepdims=True) * (1.0 / depth)
-
-        average = over_lanes(piece)
-
-        def squared(j):
-            centred = piece(j) - average
-            return centred * centred
-
-        factor = lax.rsqrt(over_lanes(squared) + 1e-06)
+        base = piece(0)[:, :1]
+        sums = [jnp.zeros((16, lanes), jnp.float32)] * 2
+        squares = [jnp.zeros((16, lanes), jnp.float32)] * 2
+        for j in range(depth // lanes):
+            away = piece(j) - base
+            sums[j % 2] = sums[j % 2] + away
+            squares[j % 2] = squares[j % 2] + away * away
+        offset = jnp.sum(sums[0] + sums[1], axis=-1, keepdims=True) * (1.0 / depth)
+        second = jnp.sum(squares[0] + squares[1], axis=-1, keepdims=True) * (1.0 / depth)
+        average = base + offset
+        factor = lax.rsqrt(jnp.maximum(second - offset * offset, 0.0) + 1e-06)
         for j in range(depth // lanes):
             part = pl.ds(j * lanes, lanes)
-            normed = (piece(j) - average) * factor * (1.0 + scale_ref[:, part]) + shift_ref[:, part]
+            normed = (piece(j) - average) * factor * affine[0, :, part] + affine[1, :, part]
             modulated[rows, part] = normed.astype(jnp.bfloat16)
         return carry
 
@@ -336,36 +339,47 @@
     bottom_keep = has_down.astype(jnp.float32)
     prev_keep = has_prev.astype(jnp.float32)
 
-    def input_rows(ci):
+    def input_product(ci, parity):
+        taps = [
+            corner[parity, a : a + EXT_F, ci + di].reshape(EXT_F * KC, width)
+            for a in range(3)
+            for di in range(2)
+        ]
+        raw = jnp.dot(
+            jnp.concatenate(taps, axis=1),
+            w_corner[:, :, 2 * chan * parity : 2 * chan * (parity + 1)].reshape(
+                6 * width, 2 * chan
+            ),
+            preferred_element_type=jnp.float32,
+        )
+        return (raw + in_bias).reshape(EXT_F, KC, 2 * chan)
+
+    def input_act(row, parity, values):
+        for f in range(EXT_F):
+            if f >= 2 and 1 <= row <= TH:
+                stream[parity, f - 2, row - 1] = values[f].astype(jnp.bfloat16)
+            keep = prev_keep if f < 2 else None
+            for edge, edge_keep in ((0, top_keep), (EXT_R - 1, bottom_keep)):
+                if row == edge:
+                    keep = edge_keep if keep is None else keep * edge_keep
+            store_act(act_one, f, row, parity, normed_silu(values[f], gain_one, keep))
+
+    for ci in range(2):
         for parity in range(2):
-            taps = [
-                corner[parity, a : a + EXT_F, ci + di].reshape(EXT_F * KC, width)
-                for a in range(3)
-                for di in range(2)
-            ]
-            raw = jnp.dot(
-                jnp.concatenate(taps, axis=1),
-                w_corner[:, :, 2 * chan * parity : 2 * chan * (parity + 1)].reshape(
-                    6 * width, 2 * chan
-                ),
-                preferred_element_type=jnp.float32,
-            )
-            raw = (raw + in_bias).reshape(EXT_F, KC, 2 * chan)
-            for f in range(EXT_F):
-                for cell in range(2):
-                    row = 2 * ci + cell
-                    values = raw[f, :, cell * chan : (cell + 1) * chan]
-                    if f >= 2 and 1 <= row <= TH:
-                        stream[parity, f - 2, row - 1] = values.astype(jnp.bfloat16)
-                    keep = prev_keep if f < 2 else None
-                    for edge, edge_keep in ((0, top_keep), (EXT_R - 1, bottom_keep)):
-                        if row == edge:
-                            keep = edge_keep if keep is None else keep * edge_keep
-                    act = normed_silu(values, gain_one, keep)
-                    store_act(act_one, f, row, parity, act)
-
-    input_rows(0)
-    input_rows(1)
+            raw = input_product(ci, parity)
+            input_act(2 * ci, parity, raw[:, :, :chan])
+            if ci == 0:
+                input_act(1, parity, raw[:, :, chan:])
+            else:
+                third[parity] = raw[:, :, chan:]
+
+    def rest_of_input():
+        for parity in range(2):
+            input_act(3, parity, third[parity])
+        for parity in range(2):
+            raw = input_product(2, parity)
+            for cell in range(2):
+                input_act(4 + cell, parity, raw[:, :, cell * chan : (cell + 1) * chan])
 
     def tap(weight, a, u, s):
         return weight[a * 9 + u * 3 + s]
@@ -483,14 +497,17 @@
             device_id_type=MESH,
         )
 
-    tm_copy = pltpu.make_async_remote_copy(
-        src_ref=act_two.at[pl.ds(EVEN, 2), pl.ds(TF, 2), pl.ds(1, TH)],
-        dst_ref=act_two.at[pl.ds(EVEN, 2), pl.ds(0, 2), pl.ds(1, TH)],
-        send_sem=tm_send.at[0],
-        recv_sem=tm_recv.at[0],
-        device_id=at(me_m + 1, me_g),
-        device_id_type=MESH,
-    )
+    def tm_copy(n):
+        rows = pl.ds((1, TH, 2)[n], (1, 1, 2)[n])
+        return pltpu.make_async_remote_copy(
+            src_ref=act_two.at[pl.ds(EVEN, 2), pl.ds(TF, 2), rows],
+            dst_ref=act_two.at[pl.ds(EVEN, 2), pl.ds(0, 2), rows],
+            send_sem=tm_send.at[n],
+            recv_sem=tm_recv.at[n],
+            device_id=at(me_m + 1, me_g),
+            device_id_type=MESH,
+        )
+
     way_out = (has_down, has_up)
     way_in = (has_up, has_down)
 
@@ -508,7 +525,7 @@
     for row, way in ((0, 1), (TH - 1, 0)):
         totals = conv(act_one, w1, own_frames, (row,), ALL_TAPS, False)
         if row == 0:
-            input_rows(2)
+            rest_of_input()
         act_two_rows(totals, (row,))
 
         @pl.when(way_out[way])
@@ -518,12 +535,16 @@
         @pl.when(way_out[way] & sends_edges)
         def _(way=way):
             edge_copy(way).start()
+
+        @pl.when(has_next)
+        def _(way=way):
+            tm_copy(1 - way).start()
 
     act_two_rows(conv(act_one, w1, own_frames, (1, 2), ALL_TAPS, True), (1, 2))
 
     @pl.when(has_next)
     def _():
-        tm_copy.start()
+        tm_copy(2).start()
 
     for copy in w_copies[1]:
         copy.wait()
@@ -553,7 +574,8 @@
 
     @pl.when(has_prev)
     def _():
-        tm_copy.wait_recv()
+        for n in range(3):
+            tm_copy(n).wait_recv()
 
     for way in range(2):
 
@@ -605,7 +627,8 @@
 
     @pl.when(has_next)
     def _():
-        tm_copy.wait_send()
+        for n in range(3):
+            tm_copy(n).wait_send()
 
     for way in range(2):
 
@@ -620,14 +643,6 @@
         @pl.when(way_in[way] & passes_edges)
         def _(way=way):
             pass_copy(way).wait_send()
-
-
-def place_kernel(held, out, sem):
-    copies = [pltpu.make_async_copy(held.at[f], out.at[f], sem.at[f]) for f in range(TF)]
-    for copy in copies:
-        copy.start()
-    for copy in copies:
-        copy.wait()
 
 
 def solution(mesh):
@@ -667,6 +682,7 @@
             scratch_shapes=[
                 pltpu.VMEM((count, depth), bf16),
                 pltpu.VMEM((count, depth), bf16),
+                pltpu.VMEM((2, 16, depth), jnp.float32),
                 pltpu.VMEM((count // KC, KC // 2, wide), bf16),
                 pltpu.VMEM((2 * TF, 4, KC // 2, wide), bf16),
                 pltpu.VMEM((2, 2 * TF, 4, KC, wide), bf16),
@@ -677,6 +693,7 @@
                 pltpu.VMEM((4, EXT_F, EXT_R, KC, chan), bf16),
                 pltpu.VMEM((4, EXT_F, EXT_R, KC, chan), bf16),
                 pltpu.VMEM((2, TF, TH, KC, chan), bf16),
+                pltpu.VMEM((2, EXT_F, KC, chan), jnp.float32),
                 pltpu.VMEM((2, 2, TH, KC, chan), jnp.float32),
                 dma((4,)),
                 dma((2, 3)),
@@ -686,8 +703,8 @@
                 dma((2 * TF,)),
                 dma((2,)),
                 dma((2,)),
-                dma((1,)),
-                dma((1,)),
+                dma((3,)),
+                dma((3,)),
                 dma((2,)),
                 dma((2,)),
             ],
@@ -710,14 +727,7 @@
             weight_two.reshape(27, chan, chan),
             bias_two,
         )
-        return pl.pallas_call(
-            place_kernel,
-            out_shape=jax.ShapeDtypeStruct(result.shape, bf16),
-            in_specs=[vmem],
-            out_specs=hbm,
-            scratch_shapes=[dma((TF,))],
-            name="place",
-        )(result)
+        return result
 
     in_specs = (P(("tm", "tile"), None), P(), P(), P(), P(), P(), P(), P(), P(), P(), P(), P(), P())
     out_specs = P("tm", "tile", None, None, None)

time: 43 us -> 42.1 us (0.979)
  the two profiles are of different devices: /device:TPU:36 before, /device:TPU:33 now
where the time goes in v4:
time: 42.1 us; the launch traced here: 41.9 us
  Pallas kernels  41 us (97%)
  local copies, waits for them, and re-layouts  0.88 us (2%)
    pallas_call x1, Pallas kernels, body(): pl.pallas_call(functools.partial(body_kernel, tiles, blocks), out_shape=p...  41 us
    unnamed x1, local copies, waits for them, and re-layouts  0.88 us

profile of v4, /device:TPU:33, one launch (start us, length us, event | category | flops | bytes accessed | tf_op | source)
XLA Modules:
  0.0 41.9 jit_solution(12125244350775257848)
XLA Ops:
  0.0 41.0 %decode.1 = bf16[4,1,64,4,384]{4,3,2,1,0:T(4,128)(2,1)S(1)} custom-call(bf16[256,5120]{1,0:T(8,128)(2,1)} %tokens.1, f32[1,5120]{1,0:T(1,128)} %bitcast.10, f32[1,5120]{1,0:T(1,128)} %bitcast.11, bf16[64,5120]{1,0:T(8,128)(2,1)} %bitcast.8, f32[64]{0:T(128)} %head_b_ref.1, bf16[432,384]{1,0:T(8,128)(2,1)} %bitcast.9, f32[384]{0:T(512)} %in_b_ref.1, ...), custom_call_target="tpu_custom_call" | custom-call | tf_op jit(solution)/shard_map/decode/pallas_call | solution.py:675
  41.0 0.9 %copy.15 = bf16[4,1,64,4,384]{4,3,2,1,0:T(4,128)(2,1)} copy(bf16[4,1,64,4,384]{4,3,2,1,0:T(4,128)(2,1)S(1)} %decode.1) | data formatting | bytes 1572864

commit v5 on v4

--- a/solution.py
+++ b/solution.py
@@ -39,6 +39,7 @@
     out_ref,
     tok,
     modulated,
+    turned_w,
     affine,
     own,
     got,
@@ -179,6 +180,8 @@
 
     lanes = 128
 
+    head_w = head_w_ref[...]
+    turned_w[...] = jnp.concatenate([head_w, head_w], axis=0).T
     affine[0] = jnp.broadcast_to(1.0 + scale_ref[...], affine.shape[1:])
     affine[1] = jnp.broadcast_to(shift_ref[...], affine.shape[1:])
 
@@ -212,13 +215,7 @@
                 copy.start()
         blocks_of = tok_rows // 16
         lax.fori_loop(i * blocks_of, (i + 1) * blocks_of, head_rows, 0, unroll=min(4, blocks_of))
-    head_w = head_w_ref[...]
-    patches = lax.dot_general(
-        modulated[...],
-        jnp.concatenate([head_w, head_w], axis=0),
-        (((1,), (1,)), ((), ())),
-        preferred_element_type=jnp.float32,
-    )
+    patches = jnp.dot(modulated[...], turned_w[...], preferred_element_type=jnp.float32)
     head_b = jnp.concatenate([row_of(head_b_ref)] * 2, axis=1)
     spread = (patches + head_b).reshape(own.shape[0], KC, own.shape[2])
     wide_left = lax.broadcasted_iota(i32, own.shape, 2) < own.shape[2] // 2
@@ -364,22 +361,27 @@
                     keep = edge_keep if keep is None else keep * edge_keep
             store_act(act_one, f, row, parity, normed_silu(values[f], gain_one, keep))
 
-    for ci in range(2):
-        for parity in range(2):
-            raw = input_product(ci, parity)
-            input_act(2 * ci, parity, raw[:, :, :chan])
-            if ci == 0:
-                input_act(1, parity, raw[:, :, chan:])
-            else:
-                third[parity] = raw[:, :, chan:]
-
-    def rest_of_input():
-        for parity in range(2):
-            input_act(3, parity, third[parity])
-        for parity in range(2):
-            raw = input_product(2, parity)
-            for cell in range(2):
-                input_act(4 + cell, parity, raw[:, :, cell * chan : (cell + 1) * chan])
+    raws = [input_product(0, parity) for parity in range(2)]
+    for parity in range(2):
+        for cell in range(2):
+            input_act(cell, parity, raws[parity][:, :, cell * chan : (cell + 1) * chan])
+        raw = input_product(1, parity)
+        third[parity] = raw[:, :, chan:]
+        raws.append(raw)
+    for parity in range(2):
+        input_act(2, parity, raws[2 + parity][:, :, :chan])
+
+    def last_rows(parity):
+        raw = input_product(2, parity)
+        for cell in range(2):
+            input_act(4 + cell, parity, raw[:, :, cell * chan : (cell + 1) * chan])
+
+    rest_of_input = (
+        lambda: input_act(3, 0, third[0]),
+        lambda: input_act(3, 1, third[1]),
+        lambda: last_rows(0),
+        lambda: last_rows(1),
+    )
 
     def tap(weight, a, u, s):
         return weight[a * 9 + u * 3 + s]
@@ -391,7 +393,7 @@
             view = [field[version, f, v + s][None] for f in frames for v in rows]
         return jnp.concatenate(view, axis=0).reshape(len(frames) * len(rows) * KC, chan)
 
-    def product(field, weight, groups, rows, taps):
+    def product(field, weight, groups, rows, taps, part=slice(None)):
         return jnp.dot(
             jnp.concatenate(
                 [cells(field, version, frames, rows, s) for version, frames, _ in groups for s in taps],
@@ -399,7 +401,7 @@
             ),
             jnp.concatenate(
                 [
-                    jnp.concatenate([tap(weight, a, u, s) for a, u in outs], axis=1)
+                    jnp.concatenate([tap(weight, a, u, s) for a, u in outs], axis=1)[:, part]
                     for _, _, outs in groups
                     for s in taps
                 ],
@@ -408,10 +410,16 @@
             preferred_element_type=jnp.float32,
         )
 
-    def conv(field, weight, frames, rows, taps, paired):
+    def conv(field, weight, frames, rows, taps, paired, sides_first, beside=()):
         shape = (len(frames), len(rows), KC, chan)
-        sides = []
-        for version, u in ((ODD_BACK, 0), (EVEN_ON, 2)):
+        calls = iter(beside)
+
+        def between():
+            call = next(calls, None)
+            if call is not None:
+                call()
+
+        def side(version, u):
             if paired:
                 firsts = frames[0::2]
                 half = (len(firsts), len(rows), KC, chan)
@@ -428,30 +436,47 @@
                 )
                 one = (one + two[:, :chan]).reshape(half)
                 other = (other + two[:, chan:]).reshape(half)
-                side = jnp.stack([one, other], axis=1)
+                total = jnp.stack([one, other], axis=1)
             else:
-                side = product(
+                total = product(
                     field,
                     weight,
                     [(version, [f + a for f in frames], ((a, u),)) for a in range(3)],
                     rows,
                     taps,
                 )
-            sides.append(side.reshape(shape))
-        both = product(
-            field,
-            weight,
-            [
-                (version, [f + a for f in frames], ((a, u + 1), (a, u)))
-                for a in range(3)
-                for version, u in ((EVEN, 0), (ODD, 1))
-            ],
-            rows,
-            taps,
-        )
-        return [
-            both[:, p * chan : (p + 1) * chan].reshape(shape) + sides[p] for p in range(2)
-        ]
+            between()
+            return total.reshape(shape)
+
+        def both(lanes):
+            total = product(
+                field,
+                weight,
+                [
+                    (version, [f + a for f in frames], ((a, u + 1), (a, u)))
+                    for a in range(3)
+                    for version, u in ((EVEN, 0), (ODD, 1))
+                ],
+                rows,
+                taps,
+                lanes,
+            )
+            between()
+            return total
+
+        cut = 4 * chan // 3
+        if sides_first:
+            even = side(ODD_BACK, 0)
+            odd = side(EVEN_ON, 2)
+        low = both(slice(0, cut))
+        if sides_first:
+            yield low[:, :chan].reshape(shape) + even
+        high = both(slice(cut, 2 * chan))
+        if not sides_first:
+            even = side(ODD_BACK, 0)
+            yield low[:, :chan].reshape(shape) + even
+            odd = side(EVEN_ON, 2)
+        yield jnp.concatenate([low[:, chan:], high], axis=1).reshape(shape) + odd
 
     gain_two = row_of(gain_two_ref) * 0.5
     bias_one = row_of(bias_one_ref)
@@ -497,17 +522,14 @@
             device_id_type=MESH,
         )
 
-    def tm_copy(n):
-        rows = pl.ds((1, TH, 2)[n], (1, 1, 2)[n])
-        return pltpu.make_async_remote_copy(
-            src_ref=act_two.at[pl.ds(EVEN, 2), pl.ds(TF, 2), rows],
-            dst_ref=act_two.at[pl.ds(EVEN, 2), pl.ds(0, 2), rows],
-            send_sem=tm_send.at[n],
-            recv_sem=tm_recv.at[n],
-            device_id=at(me_m + 1, me_g),
-            device_id_type=MESH,
-        )
-
+    tm_copy = pltpu.make_async_remote_copy(
+        src_ref=act_two.at[pl.ds(EVEN, 2), pl.ds(TF, 2), pl.ds(1, TH)],
+        dst_ref=act_two.at[pl.ds(EVEN, 2), pl.ds(0, 2), pl.ds(1, TH)],
+        send_sem=tm_send.at[0],
+        recv_sem=tm_recv.at[0],
+        device_id=at(me_m + 1, me_g),
+        device_id_type=MESH,
+    )
     way_out = (has_down, has_up)
     way_in = (has_up, has_down)
 
@@ -523,10 +545,10 @@
         copy.start()
 
     for row, way in ((0, 1), (TH - 1, 0)):
-        totals = conv(act_one, w1, own_frames, (row,), ALL_TAPS, False)
-        if row == 0:
-            rest_of_input()
-        act_two_rows(totals, (row,))
+        beside = rest_of_input if row == 0 else ()
+        act_two_rows(
+            conv(act_one, w1, own_frames, (row,), ALL_TAPS, False, True, beside), (row,)
+        )
 
         @pl.when(way_out[way])
         def _(way=way):
@@ -536,22 +558,17 @@
         def _(way=way):
             edge_copy(way).start()
 
-        @pl.when(has_next)
-        def _(way=way):
-            tm_copy(1 - way).start()
-
-    act_two_rows(conv(act_one, w1, own_frames, (1, 2), ALL_TAPS, True), (1, 2))
+    act_two_rows(conv(act_one, w1, own_frames, (1, 2), ALL_TAPS, True, True), (1, 2))
 
     @pl.when(has_next)
     def _():
-        tm_copy(2).start()
+        tm_copy.start()
 
     for copy in w_copies[1]:
         copy.wait()
 
-    totals = conv(act_two, w2, [2, 3], ALL_ROWS, (1,), True)
-    for parity in range(2):
-        acc[parity] = totals[parity] + bias_two
+    for parity, total in enumerate(conv(act_two, w2, [2, 3], ALL_ROWS, (1,), True, True)):
+        acc[parity] = total + bias_two
 
     for way in range(2):
 
@@ -563,19 +580,16 @@
         def _(way=way):
             pass_copy(way).start()
 
-        @pl.when(way_in[way])
-        def _(way=way):
-            for f in range(TF):
-                widen(2 + f, EXT_R - 1 if way else 0)
-
-    totals = conv(act_two, w2, [2, 3], ALL_ROWS, (0, 2), True)
-    for parity in range(2):
-        acc[parity] += totals[parity]
+    for row in (0, EXT_R - 1):
+        for f in range(2, EXT_F):
+            widen(f, row)
+
+    for parity, total in enumerate(conv(act_two, w2, [2, 3], ALL_ROWS, (0, 2), True, False)):
+        acc[parity] += total
 
     @pl.when(has_prev)
     def _():
-        for n in range(3):
-            tm_copy(n).wait_recv()
+        tm_copy.wait_recv()
 
     for way in range(2):
 
@@ -583,15 +597,9 @@
         def _(way=way):
             edge_copy(way).wait_recv()
 
-    @pl.when(has_prev)
-    def _():
-        for f in range(2):
-
-            def widen_row(row, carry, f=f):
-                widen(f, row)
-                return carry
-
-            lax.fori_loop(0, EXT_R, widen_row, 0, unroll=True)
+    for f in range(2):
+        for row in range(EXT_R):
+            widen(f, row)
 
     area = 2 * TH * KC
     to = lax.broadcasted_iota(i32, (area, area), 0)
@@ -612,9 +620,8 @@
         )
         out_ref[f, 0] = placed.reshape(2 * KC, TH, chan).astype(jnp.bfloat16)
 
-    totals = conv(act_two, w2, [0, 1], ALL_ROWS, ALL_TAPS, True)
-    for f in range(2):
-        finish(2 + f, [acc[p, f] for p in range(2)])
+    done = [lambda f=f: finish(2 + f, [acc[p, f] for p in range(2)]) for f in range(2)]
+    totals = list(conv(act_two, w2, [0, 1], ALL_ROWS, ALL_TAPS, True, False, done))
     for f in range(2):
         finish(f, [totals[p][f] + bias_two for p in range(2)])
 
@@ -627,8 +634,7 @@
 
     @pl.when(has_next)
     def _():
-        for n in range(3):
-            tm_copy(n).wait_send()
+        tm_copy.wait_send()
 
     for way in range(2):
 
@@ -682,6 +688,7 @@
             scratch_shapes=[
                 pltpu.VMEM((count, depth), bf16),
                 pltpu.VMEM((count, depth), bf16),
+                pltpu.VMEM((depth, wide), bf16),
                 pltpu.VMEM((2, 16, depth), jnp.float32),
                 pltpu.VMEM((count // KC, KC // 2, wide), bf16),
                 pltpu.VMEM((2 * TF, 4, KC // 2, wide), bf16),
@@ -703,8 +710,8 @@
                 dma((2 * TF,)),
                 dma((2,)),
                 dma((2,)),
-                dma((3,)),
-                dma((3,)),
+                dma((1,)),
+                dma((1,)),
                 dma((2,)),
                 dma((2,)),
             ],

time: 42.1 us -> 38.8 us (0.922)
  the two profiles are of different devices: /device:TPU:33 before, /device:TPU:36 now
where the time goes in v5:
time: 38.8 us; the launch traced here: 38.6 us
  Pallas kernels  37.7 us (97%)
  local copies, waits for them, and re-layouts  0.88 us (2%)
    pallas_call x1, Pallas kernels, body(): pl.pallas_call(functools.partial(body_kernel, tiles, blocks), out_shape=p...  37.7 us
    unnamed x1, local copies, waits for them, and re-layouts  0.88 us

profile of v5, /device:TPU:36, one launch (start us, length us, event | category | flops | bytes accessed | tf_op | source)
XLA Modules:
  0.0 38.6 jit_solution(2411786253708220876)
XLA Ops:
  0.0 37.7 %decode.1 = bf16[4,1,64,4,384]{4,3,2,1,0:T(4,128)(2,1)S(1)} custom-call(bf16[256,5120]{1,0:T(8,128)(2,1)} %tokens.1, f32[1,5120]{1,0:T(1,128)} %bitcast.10, f32[1,5120]{1,0:T(1,128)} %bitcast.11, bf16[64,5120]{1,0:T(8,128)(2,1)} %bitcast.8, f32[64]{0:T(128)} %head_b_ref.1, bf16[432,384]{1,0:T(8,128)(2,1)} %bitcast.9, f32[384]{0:T(512)} %in_b_ref.1, ...), custom_call_target="tpu_custom_call" | custom-call | tf_op jit(solution)/shard_map/decode/pallas_call | solution.py:681
  37.8 0.9 %copy.15 = bf16[4,1,64,4,384]{4,3,2,1,0:T(4,128)(2,1)} copy(bf16[4,1,64,4,384]{4,3,2,1,0:T(4,128)(2,1)S(1)} %decode.1) | data formatting | bytes 1572864

commit v6 on v5

--- a/solution.py
+++ b/solution.py
@@ -567,8 +567,19 @@
     for copy in w_copies[1]:
         copy.wait()
 
-    for parity, total in enumerate(conv(act_two, w2, [2, 3], ALL_ROWS, (1,), True, True)):
-        acc[parity] = total + bias_two
+    def add(frames, rows, totals, fresh):
+        for parity, total in enumerate(totals):
+            for n, f in enumerate(frames):
+                for i, v in enumerate(rows):
+                    base = bias_two if fresh else acc[parity, f, v]
+                    acc[parity, f, v] = base + total[n, i]
+
+    def late_frames(rows, taps, sides_first):
+        return conv(act_two, w2, [2, 3], rows, taps, False, sides_first)
+
+    edge_rows = (0, TH - 1)
+    add([2, 3], (1, 2), late_frames((1, 2), ALL_TAPS, True), True)
+    add([2, 3], edge_rows, late_frames(edge_rows, (1,), True), True)
 
     for way in range(2):
 
@@ -584,22 +595,44 @@
         for f in range(2, EXT_F):
             widen(f, row)
 
-    for parity, total in enumerate(conv(act_two, w2, [2, 3], ALL_ROWS, (0, 2), True, False)):
-        acc[parity] += total
-
-    @pl.when(has_prev)
-    def _():
-        tm_copy.wait_recv()
-
-    for way in range(2):
-
-        @pl.when(way_in[way] & has_prev)
-        def _(way=way):
-            edge_copy(way).wait_recv()
-
-    for f in range(2):
-        for row in range(EXT_R):
-            widen(f, row)
+    add([2, 3], edge_rows, late_frames(edge_rows, (0, 2), False), False)
+
+    def early_frames(own, beside):
+        calls = iter(beside)
+        full, one, one_out = ((2, [2, 3]), 2, 1) if own else ((0, [0, 1]), 1, 0)
+        single, lone = (3, 2) if own else (0, 0)
+        pair_taps = ((EVEN, 0), (ODD, 1))
+
+        def pairs(time, frames):
+            total = product(
+                act_two,
+                w2,
+                [(version, frames, ((time, u + 1), (time, u))) for version, u in pair_taps],
+                ALL_ROWS,
+                ALL_TAPS,
+            )
+            call = next(calls, None)
+            if call is not None:
+                call()
+            return total.reshape(len(frames), TH, KC, 2 * chan)
+
+        whole = pairs(*full)
+        part = pairs(1, [one])[0]
+        shape = (TH, KC, chan)
+        totals = []
+        for p, (version, u) in enumerate(((ODD_BACK, 0), (EVEN_ON, 2))):
+            times = ((2, u), (1, u)) if own else ((1, u), (0, u))
+            two = product(act_two, w2, [(version, [one], times)], ALL_ROWS, ALL_TAPS)
+            other = product(act_two, w2, [(version, [single], ((lone, u),))], ALL_ROWS, ALL_TAPS)
+            lanes = slice(p * chan, (p + 1) * chan)
+            sums = []
+            for f in range(2):
+                total = whole[f, :, :, lanes] + two[:, f * chan : (f + 1) * chan].reshape(shape)
+                if f == one_out:
+                    total = total + part[:, :, lanes] + other.reshape(shape)
+                sums.append(total)
+            totals.append(sums)
+        return totals
 
     area = 2 * TH * KC
     to = lax.broadcasted_iota(i32, (area, area), 0)
@@ -620,10 +653,28 @@
         )
         out_ref[f, 0] = placed.reshape(2 * KC, TH, chan).astype(jnp.bfloat16)
 
-    done = [lambda f=f: finish(2 + f, [acc[p, f] for p in range(2)]) for f in range(2)]
-    totals = list(conv(act_two, w2, [0, 1], ALL_ROWS, ALL_TAPS, True, False, done))
+    done = [lambda f=f: finish(2 + f, [acc[p, 2 + f] for p in range(2)]) for f in range(2)]
+    for parity, sums in enumerate(early_frames(True, done)):
+        for f in range(2):
+            acc[parity, f] = sums[f] + bias_two
+
+    @pl.when(has_prev)
+    def _():
+        tm_copy.wait_recv()
+
+    for way in range(2):
+
+        @pl.when(way_in[way] & has_prev)
+        def _(way=way):
+            edge_copy(way).wait_recv()
+
     for f in range(2):
-        finish(f, [totals[p][f] + bias_two for p in range(2)])
+        for row in range(EXT_R):
+            widen(f, row)
+
+    totals = early_frames(False, ())
+    for f in range(2):
+        finish(f, [acc[p, f] + totals[p][f] for p in range(2)])
 
     for n, (dm, d) in enumerate(sends):
         remote, copy = patch_copy(n, dm, d)
@@ -701,7 +752,7 @@
                 pltpu.VMEM((4, EXT_F, EXT_R, KC, chan), bf16),
                 pltpu.VMEM((2, TF, TH, KC, chan), bf16),
                 pltpu.VMEM((2, EXT_F, KC, chan), jnp.float32),
-                pltpu.VMEM((2, 2, TH, KC, chan), jnp.float32),
+                pltpu.VMEM((2, TF, TH, KC, chan), jnp.float32),
                 dma((4,)),
                 dma((2, 3)),
                 dma,

time: 38.8 us -> 39.1 us (level)
  the two profiles are of different devices: /device:TPU:36 before, /device:TPU:1 now
where the time goes in v6:
time: 39.1 us; the launch traced here: 39 us
  Pallas kernels  38.1 us (97%)
  local copies, waits for them, and re-layouts  0.88 us (2%)
    pallas_call x1, Pallas kernels, body(): pl.pallas_call(functools.partial(body_kernel, tiles, blocks), out_shape=p...  38.1 us
    unnamed x1, local copies, waits for them, and re-layouts  0.88 us

profile of v6, /device:TPU:1, one launch (start us, length us, event | category | flops | bytes accessed | tf_op | source)
XLA Modules:
  0.0 39.0 jit_solution(4219796348884470800)
XLA Ops:
  0.0 38.1 %decode.1 = bf16[4,1,64,4,384]{4,3,2,1,0:T(4,128)(2,1)S(1)} custom-call(bf16[256,5120]{1,0:T(8,128)(2,1)} %tokens.1, f32[1,5120]{1,0:T(1,128)} %bitcast.10, f32[1,5120]{1,0:T(1,128)} %bitcast.11, bf16[64,5120]{1,0:T(8,128)(2,1)} %bitcast.8, f32[64]{0:T(128)} %head_b_ref.1, bf16[432,384]{1,0:T(8,128)(2,1)} %bitcast.9, f32[384]{0:T(512)} %in_b_ref.1, ...), custom_call_target="tpu_custom_call" | custom-call | tf_op jit(solution)/shard_map/decode/pallas_call | solution.py:732
  38.1 0.9 %copy.15 = bf16[4,1,64,4,384]{4,3,2,1,0:T(4,128)(2,1)} copy(bf16[4,1,64,4,384]{4,3,2,1,0:T(4,128)(2,1)S(1)} %decode.1) | data formatting | bytes 1572864

commit v7 on v5

--- a/solution.py
+++ b/solution.py
@@ -78,14 +78,14 @@
     def row_of(ref):
         return ref[...].reshape(1, ref.shape[0])
 
-    tok_rows = tok.shape[0] // 4
+    tok_parts = ((0, 2), (2, 5), (5, 8))
     tok_copies = [
         pltpu.make_async_copy(
-            tokens.at[pl.ds(i * tok_rows, tok_rows)],
-            tok.at[pl.ds(i * tok_rows, tok_rows)],
+            tokens.at[pl.ds(first * KC, (last - first) * KC)],
+            tok.at[pl.ds(first * KC, (last - first) * KC)],
             tok_sem.at[i],
         )
-        for i in range(4)
+        for i, (first, last) in enumerate(tok_parts)
     ]
     in_copy = pltpu.make_async_copy(in_w, w_in, in_sem)
     w_copies = [
@@ -208,18 +208,32 @@
             modulated[rows, part] = normed.astype(jnp.bfloat16)
         return carry
 
-    for i in range(4):
+    head_b = jnp.concatenate([row_of(head_b_ref)] * 2, axis=1)
+
+    def head_part(first, last):
+        patches = jnp.dot(
+            modulated[first * KC : last * KC, :],
+            turned_w[...],
+            preferred_element_type=jnp.float32,
+        )
+        spread = (patches + head_b).reshape(last - first, KC, own.shape[2])
+        packed_shape = (last - first,) + own.shape[1:]
+        wide_left = lax.broadcasted_iota(i32, packed_shape, 2) < own.shape[2] // 2
+        own[first:last] = jnp.where(
+            wide_left, spread[:, : KC // 2], spread[:, KC // 2 :]
+        ).astype(jnp.bfloat16)
+
+    def head_tokens(i):
         tok_copies[i].wait()
-        if i == 3:
+        if i == 2:
             for copy in w_copies[0]:
                 copy.start()
-        blocks_of = tok_rows // 16
-        lax.fori_loop(i * blocks_of, (i + 1) * blocks_of, head_rows, 0, unroll=min(4, blocks_of))
-    patches = jnp.dot(modulated[...], turned_w[...], preferred_element_type=jnp.float32)
-    head_b = jnp.concatenate([row_of(head_b_ref)] * 2, axis=1)
-    spread = (patches + head_b).reshape(own.shape[0], KC, own.shape[2])
-    wide_left = lax.broadcasted_iota(i32, own.shape, 2) < own.shape[2] // 2
-    own[...] = jnp.where(wide_left, spread[:, : KC // 2], spread[:, KC // 2 :]).astype(jnp.bfloat16)
+        first, last = (n * KC // 16 for n in tok_parts[i])
+        lax.fori_loop(first, last, head_rows, 0, unroll=(last - first) // 2)
+
+    head_tokens(0)
+    head_tokens(1)
+    head_part(0, 5)
 
     def patch_copy(n, dm, d):
         m, g, remote = target(dm, d)
@@ -241,12 +255,20 @@
         count = count + here.astype(i32)
     pl.semaphore_wait(barrier, count)
 
-    for n, (dm, d) in enumerate(sends):
-        remote, copy = patch_copy(n, dm, d)
-
-        @pl.when(remote)
-        def _(copy=copy):
-            copy.start()
+    def send_patches(pieces):
+        for n, (dm, d) in enumerate(sends):
+            if d not in pieces:
+                continue
+            remote, copy = patch_copy(n, dm, d)
+
+            @pl.when(remote)
+            def _(copy=copy):
+                copy.start()
+
+    send_patches((-1, 0, 1))
+    head_tokens(2)
+    head_part(5, 8)
+    send_patches((2, 3, 4))
 
     for d, (first, size, slot) in PIECES.items():
 
@@ -702,7 +724,7 @@
                 pltpu.VMEM((2, TF, TH, KC, chan), bf16),
                 pltpu.VMEM((2, EXT_F, KC, chan), jnp.float32),
                 pltpu.VMEM((2, 2, TH, KC, chan), jnp.float32),
-                dma((4,)),
+                dma((3,)),
                 dma((2, 3)),
                 dma,
                 dma((12,)),

time: 38.8 us -> 39.5 us (1.018)
  the two profiles are of different devices: /device:TPU:36 before, /device:TPU:14 now
where the time goes in v7:
time: 39.5 us; the launch traced here: 39.4 us
  Pallas kernels  38.5 us (97%)
  local copies, waits for them, and re-layouts  0.88 us (2%)
    pallas_call x1, Pallas kernels, body(): pl.pallas_call(functools.partial(body_kernel, tiles, blocks), out_shape=p...  38.5 us
    unnamed x1, local copies, waits for them, and re-layouts  0.88 us

profile of v7, /device:TPU:14, one launch (start us, length us, event | category | flops | bytes accessed | tf_op | source)
XLA Modules:
  0.0 39.4 jit_solution(10001079634465517245)
XLA Ops:
  0.0 38.5 %decode.1 = bf16[4,1,64,4,384]{4,3,2,1,0:T(4,128)(2,1)S(1)} custom-call(bf16[256,5120]{1,0:T(8,128)(2,1)} %tokens.1, f32[1,5120]{1,0:T(1,128)} %bitcast.10, f32[1,5120]{1,0:T(1,128)} %bitcast.11, bf16[64,5120]{1,0:T(8,128)(2,1)} %bitcast.8, f32[64]{0:T(128)} %head_b_ref.1, bf16[432,384]{1,0:T(8,128)(2,1)} %bitcast.9, f32[384]{0:T(512)} %in_b_ref.1, ...), custom_call_target="tpu_custom_call" | custom-call | tf_op jit(solution)/shard_map/decode/pallas_call | solution.py:703
  38.5 0.9 %copy.15 = bf16[4,1,64,4,384]{4,3,2,1,0:T(4,128)(2,1)} copy(bf16[4,1,64,4,384]{4,3,2,1,0:T(4,128)(2,1)S(1)} %decode.1) | data formatting | bytes 1572864

commit v8 on v5

--- a/solution.py
+++ b/solution.py
@@ -376,12 +376,11 @@
         for cell in range(2):
             input_act(4 + cell, parity, raw[:, :, cell * chan : (cell + 1) * chan])
 
-    rest_of_input = (
-        lambda: input_act(3, 0, third[0]),
-        lambda: input_act(3, 1, third[1]),
-        lambda: last_rows(0),
-        lambda: last_rows(1),
-    )
+    def fourth_row():
+        for parity in range(2):
+            input_act(3, parity, third[parity])
+
+    rest_of_input = (lambda: last_rows(0), lambda: last_rows(1), fourth_row)
 
     def tap(weight, a, u, s):
         return weight[a * 9 + u * 3 + s]
@@ -483,12 +482,15 @@
     bias_two = row_of(bias_two_ref)
     own_frames = list(range(TF))
 
+    def act_two_part(total, rows, parity):
+        for f in range(TF):
+            for i, v in enumerate(rows):
+                act = normed_silu(total[f, i] + bias_one, gain_two)
+                store_act(act_two, f + 2, v + 1, parity, act)
+
     def act_two_rows(totals, rows):
         for parity, total in enumerate(totals):
-            for f in range(TF):
-                for i, v in enumerate(rows):
-                    act = normed_silu(total[f, i] + bias_one, gain_two)
-                    store_act(act_two, f + 2, v + 1, parity, act)
+            act_two_part(total, rows, parity)
 
     def row_copy(way):
         frames = pl.ds(2, TF)
@@ -558,17 +560,26 @@
         def _(way=way):
             edge_copy(way).start()
 
-    act_two_rows(conv(act_one, w1, own_frames, (1, 2), ALL_TAPS, True, True), (1, 2))
+    for copy in w_copies[1]:
+        copy.wait()
+
+    def along_rows(rows, beside=()):
+        totals = conv(act_two, w2, [2, 3], rows, (1,), False, True, beside)
+        for parity, total in enumerate(totals):
+            for i, v in enumerate(rows):
+                acc[parity, :, v] = total[:, i] + bias_two
+
+    middle = (1, 2)
+    totals = conv(act_one, w1, own_frames, middle, ALL_TAPS, True, True)
+    act_two_part(next(totals), middle, 0)
+    odd_total = next(totals)
+    along_rows((0, TH - 1), [lambda: act_two_part(odd_total, middle, 1)])
 
     @pl.when(has_next)
     def _():
         tm_copy.start()
 
-    for copy in w_copies[1]:
-        copy.wait()
-
-    for parity, total in enumerate(conv(act_two, w2, [2, 3], ALL_ROWS, (1,), True, True)):
-        acc[parity] = total + bias_two
+    along_rows(middle)
 
     for way in range(2):
 

time: 38.8 us -> 39.6 us (1.021)
  Pallas kernels: 37.7 us -> 38.2 us
    pallas_call x1, Pallas kernels: 37.7 us -> 38.2 us  [body(): pl.pallas_call(functools.partial(body_kernel, tiles, blocks), out_shape=p...]
where the time goes in v8:
time: 39.6 us; the launch traced here: 39 us
  Pallas kernels  38.2 us (96%)
  local copies, waits for them, and re-layouts  0.88 us (2%)
    pallas_call x1, Pallas kernels, body(): pl.pallas_call(functools.partial(body_kernel, tiles, blocks), out_shape=p...  38.2 us
    unnamed x1, local copies, waits for them, and re-layouts  0.88 us

profile of v8, /device:TPU:36, one launch (start us, length us, event | category | flops | bytes accessed | tf_op | source)
XLA Modules:
  0.0 39.0 jit_solution(3387108292748824558)
XLA Ops:
  0.0 38.2 %decode.1 = bf16[4,1,64,4,384]{4,3,2,1,0:T(4,128)(2,1)S(1)} custom-call(bf16[256,5120]{1,0:T(8,128)(2,1)} %tokens.1, f32[1,5120]{1,0:T(1,128)} %bitcast.10, f32[1,5120]{1,0:T(1,128)} %bitcast.11, bf16[64,5120]{1,0:T(8,128)(2,1)} %bitcast.8, f32[64]{0:T(128)} %head_b_ref.1, bf16[432,384]{1,0:T(8,128)(2,1)} %bitcast.9, f32[384]{0:T(512)} %in_b_ref.1, ...), custom_call_target="tpu_custom_call" | custom-call | tf_op jit(solution)/shard_map/decode/pallas_call | solution.py:692
  38.2 0.9 %copy.15 = bf16[4,1,64,4,384]{4,3,2,1,0:T(4,128)(2,1)} copy(bf16[4,1,64,4,384]{4,3,2,1,0:T(4,128)(2,1)S(1)} %decode.1) | data formatting | bytes 1572864
